TPU v7x, 256 devices: a whole 4x4x8 slice. The times are simulated.
256 devices in a mesh: region: 8 (over z), dev: 32 (over y, x, core).
Axes of the slice: x: 4, y: 4, z: 8, core: 2. Of those that a mesh axis runs over, the one named last changes fastest.
Arguments:
- probes: float32 [512, 8, 512], P(('region', 'dev')), may hold values from -20 to 20
- coords: float32 [512, 3, 512], P(('region', 'dev')), may hold values from 0 to 1
- features: float32 [512, 16, 512], P(('region', 'dev')), may hold values from -1 to 1
- noise_var: float32 [512, 512], P(('region', 'dev')), may hold values from 0.5 to 2
- inv_scale: float32 [3], replicated, may hold values from 1.2 to 2.4
- owner_map: int32 [8, 64], P('region'), may hold values from 0 to 63, as said below
- block_pairs: int32 [8, 64, 2], P('region'), may hold values from 0 to 63, as said below
Outputs:
- solution: float32 [512, 8, 512], P(('region', 'dev'))
- residual: float32 [512, 8, 512], P(('region', 'dev'))
Inputs may be any that keep to these rules, and one draw needn't show every extreme that they name: `owner_map`: each region group's row is a permutation of 0 to 63. `block_pairs`: each region group's 64 rows are pairs of two blocks of that group. With a block's device in its group taken as its slot in the group // 2, the two blocks of a pair lie on different devices, and no two listed pairs of a group join the same two devices.
All inputs are finite; a program needn't handle non-finite values.
Results may differ from a plain program's by a relative error of at most 0.00013.
Values sent between devices are 32-bit elements; how exact they have to be, the bound alone decides.
A program may use at most 64 MiB of HBM per device.

v0:
```python
import jax
import jax.numpy as jnp
from jax import lax
from jax.sharding import PartitionSpec as P

ITERS = 2


FULL_PRECISION = lax.Precision.HIGHEST


def wendland(radius):
    inside = jnp.maximum(1.0 - radius, 0.0)
    return inside * inside * inside * inside * (4.0 * radius + 1.0)


def kernel_tile(left_points, right_points, inv_scale):
    delta_x = (left_points[0][:, None] - right_points[0][None, :]) * inv_scale[0]
    delta_y = (left_points[1][:, None] - right_points[1][None, :]) * inv_scale[1]
    delta_t = jnp.abs(left_points[2][:, None] - right_points[2][None, :]) * inv_scale[2]
    spatial = jnp.sqrt(delta_x * delta_x + delta_y * delta_y)
    return 0.25 * wendland(spatial) * wendland(delta_t)


def apply_tile(kernel_block, vectors):
    return jnp.einsum("ab,cb->ca", kernel_block, vectors, precision=FULL_PRECISION)


def column_sum(left_vec, right_vec):
    return jnp.sum(left_vec * right_vec, axis=(0, 2))


def squares_plain(vectors):
    return lax.psum(column_sum(vectors, vectors), ("region", "dev"))


def shards(probes, coords, features, noise_var, inv_scale, owner_map, block_pairs):
    my_index = lax.axis_index("dev")
    group_size = lax.axis_size("dev")
    my_blocks = probes.shape[0]
    slot_pairs = owner_map[0][block_pairs[0]]
    near_side = jnp.concatenate([slot_pairs[:, 0], slot_pairs[:, 1]])
    far_side = jnp.concatenate([slot_pairs[:, 1], slot_pairs[:, 0]])
    first_owned = my_index * my_blocks
    local_ids = first_owned + jnp.arange(my_blocks, dtype=jnp.int32)
    appear = jnp.sum((near_side[None, :] == local_ids[:, None]).astype(jnp.float32), axis=1)
    multiple = 1.0 + appear
    owned_flag = near_side // my_blocks == my_index
    sort_key = jnp.where(owned_flag, far_side, group_size * my_blocks)
    ordering = jnp.argsort(sort_key)
    sorted_key = sort_key[ordering]
    sorted_near = near_side[ordering] - first_owned
    solution = jnp.zeros_like(probes)
    residual = probes
    direction = probes
    norm_now = squares_plain(residual)
    for sweep_index in range(ITERS):

        def one_block(operand_set):
            block_points, block_vectors, factor = operand_set
            return factor * apply_tile(
                kernel_tile(block_points, block_points, inv_scale), block_vectors
            )

        own_terms = (
            lax.map(one_block, (coords, direction, multiple)) + noise_var[:, None, :] * direction
        )
        zero_sum = jnp.zeros(direction.shape, jnp.float32)
        first_row = jnp.int32(0)
        piece_vectors = lax.all_gather(direction, "dev", axis=0, tiled=True)
        piece_points = lax.all_gather(coords, "dev", axis=0, tiled=True)
        row_count = piece_vectors.shape[0]
        lower_end = jnp.sum((sorted_key < first_row).astype(jnp.int32))
        upper_end = jnp.sum((sorted_key < first_row + row_count).astype(jnp.int32))

        def visit_entry(entry_index, running):
            local_block = sorted_near[entry_index]
            remote_block = sorted_key[entry_index]
            kernel_block = kernel_tile(
                lax.dynamic_index_in_dim(coords, local_block, 0, keepdims=False),
                lax.dynamic_index_in_dim(piece_points, remote_block, 0, keepdims=False),
                inv_scale,
            )
            contribution = apply_tile(
                kernel_block,
                lax.dynamic_index_in_dim(piece_vectors, remote_block, 0, keepdims=False),
            )
            current = lax.dynamic_index_in_dim(running, local_block, 0, keepdims=False)
            return lax.dynamic_update_index_in_dim(running, current + contribution, local_block, 0)

        coupled = lax.fori_loop(lower_end, upper_end, visit_entry, zero_sum)
        feature_load = jnp.einsum("bfn,bcn->fc", features, direction, precision=FULL_PRECISION)
        local_image, feature_load = (own_terms + coupled, feature_load)
        feature_sums = lax.psum(feature_load, ("region", "dev"))
        image_vec = local_image + jnp.einsum(
            "bfn,fc->bcn", features, feature_sums, precision=FULL_PRECISION
        )
        curvature = lax.psum(column_sum(direction, image_vec), ("region", "dev"))
        step_size = norm_now / curvature
        solution = solution + step_size[None, :, None] * direction
        residual = residual - step_size[None, :, None] * image_vec
        if sweep_index + 1 < ITERS:
            norm_next = squares_plain(residual)
            direction = residual + (norm_next / norm_now)[None, :, None] * direction
            norm_now = norm_next
    return (solution, residual)


def solution(mesh):
    return jax.shard_map(
        shards,
        mesh=mesh,
        in_specs=(
            P(("region", "dev"), None, None),
            P(("region", "dev"), None, None),
            P(("region", "dev"), None, None),
            P(("region", "dev"), None),
            P(),
            P("region", None),
            P("region", None, None),
        ),
        out_specs=(P(("region", "dev"), None, None), P(("region", "dev"), None, None)),
        check_vma=False,
    )
```

profile of v0, /device:TPU:1, one launch (start us, length us, event | category | flops | bytes accessed | tf_op | source)
XLA Modules:
  0.0 876.6 jit_solution(10589542826826757438)
XLA Ops:
  9.5 1.2 gather_fusion
  11.2 2.5 sort.17
  13.7 1.2 gather_fusion.1
  15.0 1.2 gather_fusion.2
  16.2 0.7 fusion.194
  17.7 81.8 %psum.43 = f32[16,8]{0,1:T(8,128)S(1)} all-reduce(f32[16,8]{0,1:T(8,128)S(1)} %convolution_bitcast_fusion.3), channel_id=1, replica_groups=mesh['region'=8,'dev'=32] {'region','dev'}, use_global_device_ids=true, to_apply=%region_10.11 | all-reduce | flops 128 | bytes 1024 | tf_op jit(solution)/shard_map/psum | solution.py:94
  99.4 23.1 %all_gather.11 = f32[64,3,512]{2,1,0:T(4,128)S(1)} all-gather(f32[2,3,512]{2,1,0:T(4,128)S(1)} %copy.16), channel_id=1, replica_groups=mesh['region'=8,'dev'=32] {'dev'}, dimensions={0}, use_global_device_ids=true | all-gather | bytes 405504 | tf_op jit(solution)/shard_map/all_gather | solution.py:71
  123.4 11.9 %while.40 = (s32[]{:T(128)}, f32[2,8,512]{2,1,0:T(8,128)S(1)}, f32[2]{0:T(128)S(1)}, f32[2,8,512]{2,1,0:T(8,128)S(1)}, f32[2,3,512]{2,0,1:T(2,128)S(1)}, /*index...) while((s32[]{:T(128)}, f32[2,8,512]{2,1,0:T(8,128)S(1)}, f32[2]{0:T(128)S(1)}, f32[2,8,512]{2,1,0:T(8,128)S(1)}, ...), condition=%wide.region_4.5_spmd, body=%wide.region_3.4_spmd.sunk | while | flops 32509956 | bytes 58565 | solution.py:66
  124.7 4.6 fusion.224
  130.7 4.6 fusion.224
  135.3 22.7 %while.41 = (s32[]{:T(128)}, f32[2,8,512]{2,1,0:T(8,128)S(1)}, s32[]{:T(128)}, s32[128]{0:T(128)S(1)}, s32[128]{0:T(128)S(1)}, /*index=5*/f32[64,8,512]{2,1,0:T(...) while((s32[]{:T(128)}, f32[2,8,512]{2,1,0:T(8,128)S(1)}, ...), condition=%wide.region_9.10_spmd, body=%wide.region_8.9_spmd.sunk | while | flops 32509964 | bytes 120687 | solution.py:91
  141.6 4.7 fusion.228
  152.6 4.7 fusion.228
  158.3 246.3 %all-reduce = (f32[8]{0:T(128)S(1)}, f32[8]{0:T(128)S(1)}) all-reduce(f32[8]{0:T(128)S(1)} %get-tuple-element.169, f32[8]{0:T(128)S(1)} %get-tuple-element.168), channel_id=1, replica_groups=mesh['region'=8,'dev'=32] {'region','dev'}, use_global_device_ids=true, to_apply=%region_1.2 | all-reduce | flops 16 | bytes 128 | tf_op jit(solution)/shard_map/psum | solution.py:34
  404.8 73.8 %psum.45 = f32[8]{0:T(128)S(1)} all-reduce(f32[8]{0:T(128)S(1)} %multiply_reduce_fusion.1), channel_id=1, replica_groups=mesh['region'=8,'dev'=32] {'region','dev'}, use_global_device_ids=true, to_apply=%region_14.15 | all-reduce | flops 8 | bytes 64 | tf_op jit(solution)/shard_map/psum | solution.py:34
  479.3 0.7 copy-done.5
  480.2 74.2 %psum.46 = f32[16,8]{0,1:T(8,128)S(1)} all-reduce(f32[16,8]{0,1:T(8,128)S(1)} %convolution_bitcast_fusion.2), channel_id=1, replica_groups=mesh['region'=8,'dev'=32] {'region','dev'}, use_global_device_ids=true, to_apply=%region_19.20 | all-reduce | flops 128 | bytes 1024 | tf_op jit(solution)/shard_map/psum | solution.py:94
  554.4 11.9 %while.42 = (s32[]{:T(128)}, f32[2,8,512]{2,1,0:T(8,128)S(1)}, f32[2]{0:T(128)S(1)}, f32[2,8,512]{2,1,0:T(8,128)S(1)}, f32[2,3,512]{2,0,1:T(2,128)S(1)}, /*index...) while((s32[]{:T(128)}, f32[2,8,512]{2,1,0:T(8,128)S(1)}, f32[2]{0:T(128)S(1)}, ...), condition=%wide.region_16.17_spmd, body=%wide.region_15.16_spmd.sunk | while | flops 32509956 | bytes 58565 | solution.py:66
  555.8 4.6 fusion.232
  561.7 4.6 fusion.232
  566.4 27.0 %while.43 = (s32[]{:T(128)}, f32[2,8,512]{2,1,0:T(8,128)S(1)}, s32[]{:T(128)}, s32[128]{0:T(128)S(1)}, s32[128]{0:T(128)S(1)}, /*index=5*/f32[64,8,512]{2,1,0:T(...) while((s32[]{:T(128)}, f32[2,8,512]{2,1,0:T(8,128)S(1)}, ...), condition=%wide.region_18.19_spmd, body=%wide.region_17.18_spmd.sunk | while | flops 32509964 | bytes 120687 | solution.py:91
  574.0 4.8 fusion.236
  586.8 4.8 fusion.236
  593.7 275.4 %psum.47 = f32[8]{0:T(128)S(1)} all-reduce(f32[8]{0:T(128)S(1)} %get-tuple-element.271), channel_id=1, replica_groups=mesh['region'=8,'dev'=32] {'region','dev'}, use_global_device_ids=true, to_apply=%region_21.22 | all-reduce | flops 8 | bytes 64 | tf_op jit(solution)/shard_map/psum | solution.py:98
  (85 shorter events, 18.8 us)
Async XLA Ops:
  7.2 10.3 %copy-start = (f32[2,16,512]{2,1,0:T(8,128)S(1)}, f32[2,16,512]{2,1,0:T(8,128)}, u32[]{:S(2)}) copy-start(f32[2,16,512]{2,1,0:T(8,128)} %param.17) | copy-start | bytes 196612
  7.2 128.1 %all-gather.3.cloned.1.call-start = ((), (), s32[]{:S(2)}) async-start(), calls=%async_computation | async-start | bytes 1081344 | tf_op jit(solution)/shard_map/all_gather | solution.py:70
  7.9 0.7 copy-start.7
  7.9 558.4 %all-gather.5.cloned.1.call-start = ((), (), s32[]{:S(2)}) async-start(), calls=%async_computation.1 | async-start | bytes 1081344 | tf_op jit(solution)/shard_map/all_gather | solution.py:70
  8.8 0.7 copy-start.1
  14.9 2.5 copy-start.3
  16.2 1.3 copy-start.4
  122.7 0.7 copy-start.2
  135.3 22.7 %copy-start.6 = (f32[2,512]{1,0:T(2,128)S(1)}, f32[2,512]{1,0:T(2,128)}, u32[]{:S(2)}) copy-start(f32[2,512]{1,0:T(2,128)} %param.18) | copy-start | bytes 12292
  479.3 0.8 copy-start.5
Sparse Core Ops, SparseCore 0:
  10.6 52.0 all-gather.2
  479.4 44.1 all-gather.4
where the time goes:
time: 883 us; the launch traced here: 877 us
  blocking collectives  775 us (88%)
  matrix products  38.4 us (4%)
  loops' own time  23.2 us (3%)
  local copies, waits for them, and re-layouts  19.7 us (2%)
  between operations  14.8 us (2%)
    psum x2, blocking collectives, squares_plain(): return lax.psum(column_sum(vectors, vectors), ('region', 'dev'))  320 us
    psum x1, blocking collectives, shards(): curvature = lax.psum(column_sum(direction, image_vec), ('region', 'dev'))  275 us
    psum x2, blocking collectives, shards(): feature_sums = lax.psum(feature_load, ('region', 'dev'))  156 us
    dot_general x8, matrix products, apply_tile(): jnp.einsum('ab,cb->ca', kernel_block, vectors, precision=FULL_PRECISION)  37.6 us
    another operation x2, loops' own time, shards(): coupled = lax.fori_loop(lower_end, upper_end, visit_entry, zero_sum)  23.2 us
    all_gather x1, blocking collectives, shards(): piece_points = lax.all_gather(coords, 'dev', axis=0, tiled=True)  23.1 us
  transfers between devices with their start and end apart: 2, of which 0 were waited for; matrix products, arithmetic and copies ran while one was open for 4% of the time, Pallas kernels for 0%

commit v1 on v0

v1 whole, which is shorter than its diff:
```python
import functools

import jax
import jax.numpy as jnp
from jax import lax
from jax.experimental import pallas as pl
from jax.experimental.pallas import tpu as pltpu
from jax.sharding import PartitionSpec as P

MESH = pl.DeviceIdType.MESH
HIGH = lax.Precision.HIGHEST
F32 = jnp.float32
BF16 = jnp.bfloat16
BLK = 512
NT = (((1,), (1,)), ((), ()))
NN = (((1,), (0,)), ((), ()))


def kernel(
    probes, coords, features, noise, inv_scale, owner_s, pairs_s, owner_v, pairs_v,
    out_sol, out_res,
    stage, sib_feat, v1, v2, v3, kh, kl, turned, quad, w2m, w3m, diag, targets, ax, ay, az, fin, fin_sib,
    s1_send, s1_recv, sib_send, sib_recv, ag_send, ag_recv, ar_send, ar_recv, fin_send, fin_recv,
):
    region = lax.axis_index("region")
    dev = lax.axis_index("dev")
    y, x, core = dev // 8, (dev // 2) % 4, dev % 2
    chip = y * 4 + x
    pos = (chip, x * 4 + y)

    def at(yy, xx, cc):
        return (region, yy * 8 + xx * 2 + cc)

    def x_peer(d, cc):
        return at(y, lax.rem(x + d, 4), cc)

    def y_peer(d, cc):
        return at(lax.rem(y + d, 4), x, cc)

    def z_peer(d):
        return (lax.rem(region + d, 8), dev)

    sibling = at(y, x, 1 - core)
    along = (x_peer, y_peer)

    barrier = pltpu.get_barrier_semaphore()
    for d in (1, 2, 3):
        for cc in (0, 1):
            pl.semaphore_signal(barrier, inc=1, device_id=x_peer(d, cc), device_id_type=MESH)
            pl.semaphore_signal(barrier, inc=1, device_id=y_peer(d, cc), device_id_type=MESH)
    pl.semaphore_signal(barrier, inc=1, device_id=sibling, device_id_type=MESH)
    for d in range(1, 8):
        pl.semaphore_signal(barrier, inc=1, device_id=z_peer(d), device_id_type=MESH)

    row = lax.broadcasted_iota(jnp.int32, (8, BLK), 0)
    low = row < 4
    for b in (0, 1):
        block = probes[b]
        for cc in (0, 1):
            stage[cc, b] = block if cc == 0 else pltpu.roll(block, 4, 0)
            stage[cc, b, 4:7, :] = coords[b]
            stage[cc, b, 7:8, :] = noise[b : b + 1, :]
        v1[b * 32 + pos[b] * 2 + core] = stage[core, b]

    pl.semaphore_wait(barrier, 20)

    def copy(src, dst, ssem, rsem, device):
        return pltpu.make_async_remote_copy(
            src_ref=src, dst_ref=dst, send_sem=ssem, recv_sem=rsem, device_id=device, device_id_type=MESH
        )

    sends = []
    feat_copy = copy(features, sib_feat, sib_send.at[2], sib_recv.at[2], sibling)
    sib_copies = []
    for b in (0, 1):
        own = v1.at[b * 32 + pos[b] * 2 + core]
        c = copy(stage.at[1 - core, b], own, sib_send.at[b], sib_recv.at[b], sibling)
        c.start()
        sib_copies.append(c)
        for d in (1, 2, 3):
            for cc in (0, 1):
                c = copy(stage.at[cc, b], own, s1_send.at[b, d - 1, cc], s1_recv.at[b, d - 1, core], along[b](d, cc))
                c.start()
                sends.append(c)
    feat_copy.start()

    def gather_copies(buf, m, stage_index, call):
        out = []
        for h in (0, 1):
            if stage_index == 0:
                span = pl.ds(h * 16 * m + pos[h] * m, m)
                peer = along[h]
            else:
                span = pl.ds(h * 16 * m + (y, x)[h] * 4 * m, 4 * m)
                peer = along[1 - h]
            for d in (1, 2, 3):
                sem = (call, stage_index, h, d - 1)
                out.append(copy(buf.at[span], buf.at[span], ag_send.at[sem], ag_recv.at[sem], peer(d, core)))
        return out

    def start_all(copies):
        for c in copies:
            c.start()
            sends.append(c)

    def arrive_all(copies):
        for c in copies:
            c.wait_recv()

    sx, sy, st = inv_scale[0], inv_scale[1], inv_scale[2]

    def make_tile(index, left, right):
        turned[...] = jnp.transpose(left)
        rx, ry, rt = right[4:5, :] * sx, right[5:6, :] * sy, right[6:7, :] * st

        def rows(i, _):
            span = pl.ds(pl.multiple_of(i * 16, 16), 16)
            part = turned[span, :]
            dx = part[:, 4:5] * sx - rx
            dy = part[:, 5:6] * sy - ry
            dt = part[:, 6:7] * st - rt
            sq = jnp.maximum(dx * dx + dy * dy, 1e-30)
            a = jnp.maximum(1.0 - sq * lax.rsqrt(sq), 0.0)
            b = jnp.maximum(1.0 - jnp.abs(dt), 0.0)
            m = a * b
            m = m * m
            m = m * m
            value = m * ((1.25 - a) * (1.25 - b))
            high = value.astype(BF16)
            kh[index, span, :] = high
            kl[index, span, :] = (value - high.astype(F32)).astype(BF16)
            return 0

        lax.fori_loop(0, 32, rows, 0, unroll=4)

    def twice(v):
        return jnp.where(low, v, pltpu.roll(v, 4, 0))

    def split(v):
        high = v.astype(BF16).astype(F32)
        return jnp.where(low, high, v - high).astype(BF16)

    def apply(v, index, dims):
        s = lax.dot_general(v, kh[index], dims, preferred_element_type=F32)
        s = s + lax.dot_general(v, kl[index], dims, preferred_element_type=F32)
        return 4.0 * (s + pltpu.roll(s, 4, 0))

    def local_slot(k):
        return (k % 2) * 32 + pos[k % 2] * 2 + k // 2

    lane64 = lax.broadcasted_iota(jnp.int32, (64, 64), 1)
    owner_row = owner_v[...].astype(F32)
    ids = pairs_v[0]
    slot_a = jnp.sum(jnp.where(ids[:, 0:1] == lane64, owner_row, 0.0), axis=1, keepdims=True)
    slot_b = jnp.sum(jnp.where(ids[:, 1:2] == lane64, owner_row, 0.0), axis=1, keepdims=True)
    first, second = [], []
    for i in range(4):
        first.append(owner_s[0, pairs_s[0, chip * 4 + i, 0]])
        second.append(owner_s[0, pairs_s[0, chip * 4 + i, 1]])

    def lane_slots(m):
        width = 2 * 16 * m * 8
        j = lax.broadcasted_iota(jnp.int32, (1, width), 1)
        n = j >> 3
        side = (j >> 2) & 1
        h = (n >= 16 * m).astype(jnp.int32)
        rest = n - h * 16 * m
        place = (rest * 171) >> 9 if m == 3 else rest >> 1
        e = rest - place * m
        q = jnp.where(h == 0, place, (place & 3) * 4 + (place >> 2))
        p = q * 4 + h * 2 + e
        pick = lax.broadcasted_iota(jnp.int32, (64, width), 0) == p
        listed = jnp.sum(jnp.where(pick, jnp.where(side == 0, slot_a, slot_b), 0.0), axis=0, keepdims=True)
        own = (q * 4 + side * 2 + h).astype(F32)
        return jnp.where(e == 2, own, listed), j & 3

    def choose(width, lanes, column, slot):
        r = lax.broadcasted_iota(jnp.int32, (8, width), 0) & 3
        hit = (lanes == slot.astype(F32)) & (r == column)
        return jnp.where(hit, 1.0, 0.0)

    lanes2, column2 = lane_slots(3)
    lanes3, column3 = lane_slots(2)
    wanted = []
    for i in range(4):
        wanted += [first[i], second[i]]
    for k in range(4):
        wanted.append(chip * 4 + k)
    for k in range(12):
        w2m[8 * k : 8 * k + 8, :] = choose(768, lanes2, column2, wanted[k])
    factor = []
    for k in range(4):
        w3m[8 * k : 8 * k + 8, :] = choose(512, lanes3, column3, wanted[8 + k])
        me = wanted[8 + k].astype(F32)
        count = jnp.where(slot_a == me, 1.0, 0.0) + jnp.where(slot_b == me, 1.0, 0.0)
        factor.append(1.0 + jnp.sum(count, axis=0, keepdims=True))

    for b in (0, 1):
        mine = stage[0, b]
        make_tile(2 * core + b, mine, mine)

    for b in (0, 1):
        sib_copies[b].wait_recv()
        for d in (1, 2, 3):
            for cc in (0, 1):
                copy(
                    stage.at[cc, b], v1.at[b * 32 + pos[b] * 2 + core], s1_send.at[b, d - 1, cc],
                    s1_recv.at[b, d - 1, cc], along[b](d, cc),
                ).wait_recv()
    second_stage = gather_copies(v1, 2, 1, 0)
    start_all(second_stage)

    feat_copy.wait_recv()
    quad[...] = jnp.zeros_like(quad)
    for k in range(4):
        here = jnp.where(core == k // 2, features[k % 2], sib_feat[k % 2])
        quad[k, 0:16, :] = here
        quad[k, 16:24, :] = v1[local_slot(k)]

    def wave(call, stage_index, buf, me, peer, count, value):
        buf[call, me] = value
        copies = []
        for d in range(1, count):
            sem = (call, stage_index, d - 1)
            copies.append(copy(buf.at[call, me], buf.at[call, me], ar_send.at[sem], ar_recv.at[sem], peer(d)))
        start_all(copies)
        return copies

    def total(call, buf, count, copies):
        arrive_all(copies)
        t = buf[call, 0]
        for i in range(1, count):
            t = t + buf[call, i]
        return t

    xp, yp = (lambda d: x_peer(d, core)), (lambda d: y_peer(d, core))

    def loads(values):
        t = jnp.zeros((8, 128), F32)
        for k in range(4):
            t = t + lax.dot_general(values(k), quad[k], NT, precision=HIGH, preferred_element_type=F32)
        return t

    wx = wave(0, 0, ax, x, xp, 4, loads(lambda k: v1[local_slot(k)]))

    for b in (0, 1):
        theirs = v1[b * 32 + pos[b] * 2 + (1 - core)]
        make_tile(2 * (1 - core) + b, theirs, theirs)
    wy = wave(0, 1, ay, y, yp, 4, total(0, ax, 4, wx))
    for k in range(4):
        mine = twice(v1[local_slot(k)])
        diag[k] = factor[k] * apply(split(mine), k, NN) + quad[k, 23:24, :] * mine
    wz = wave(0, 2, az, region, z_peer, 8, total(0, ay, 4, wy))

    arrive_all(second_stage)

    def flat(s):
        q = s >> 2
        b = s & 1
        place = jnp.where(b == 0, q, (q & 3) * 4 + (q >> 2))
        return b * 32 + place * 2 + ((s >> 1) & 1)

    for i in range(4):
        va, vb = v1[flat(first[i])], v1[flat(second[i])]
        make_tile(4 + i, va, vb)
        ya = apply(split(twice(vb)), 4 + i, NT)
        yb = apply(split(twice(va)), 4 + i, NN)
        h = i // 2
        v2[h * 48 + pos[h] * 3 + i % 2] = jnp.where(low, ya, yb)

    lane = lax.broadcasted_iota(jnp.int32, (8, 128), 1)
    row128 = lax.broadcasted_iota(jnp.int32, (8, 128), 0)
    sums1 = total(0, az, 8, wz)

    def spread(sums, k):
        g = jnp.where(lane < 16, sums, 0.0)
        return twice(lax.dot_general(g, quad[k], NN, precision=HIGH, preferred_element_type=F32))

    for b in (0, 1):
        d0 = diag[b] + spread(sums1, b)
        d1 = diag[2 + b] + spread(sums1, 2 + b)
        v2[b * 48 + pos[b] * 3 + 2] = jnp.where(low, d0, d1)

    copies = gather_copies(v2, 3, 0, 1)
    start_all(copies)
    arrive_all(copies)
    copies = gather_copies(v2, 3, 1, 1)
    start_all(copies)
    arrive_all(copies)

    def combine(weights, buf, rows):
        acc = None
        for lo_row in range(0, rows, 256):
            part = buf[lo_row // 8 : lo_row // 8 + 32].reshape(256, BLK)
            w = weights[:, lo_row : lo_row + 256].astype(BF16)
            high = part.astype(BF16)
            rest = (part - high.astype(F32)).astype(BF16)
            s = lax.dot_general(w, high, NN, preferred_element_type=F32)
            s = s + lax.dot_general(w, rest, NN, preferred_element_type=F32)
            acc = s if acc is None else acc + s
        return acc

    targets[...] = combine(w2m, v2, 768).reshape(12, 8, BLK)

    form = jnp.zeros((8, BLK), F32)
    for i in range(4):
        wa, wb = targets[2 * i], targets[2 * i + 1]
        ya = apply(split(wb), 4 + i, NT)
        yb = apply(split(wa), 4 + i, NN)
        h = i // 2
        v3[h * 32 + pos[h] * 2 + i % 2] = jnp.where(low, ya, yb)
        form = form + 2.0 * (wa * ya)
    copies3 = gather_copies(v3, 2, 0, 2)
    start_all(copies3)
    for k in range(4):
        mine = targets[8 + k]
        z = factor[k] * apply(split(mine), k, NN) + quad[k, 23:24, :] * mine
        diag[k] = z
        form = form + mine * z
        quad[k, 20:24, :] = mine[0:4, :]
    sums = loads(lambda k: targets[8 + k])
    sums = jnp.where(lane == 24, jnp.sum(form, axis=1, keepdims=True), sums)
    wx = wave(1, 0, ax, x, xp, 4, sums)
    wy = wave(1, 1, ay, y, yp, 4, total(1, ax, 4, wx))
    arrive_all(copies3)
    copies3 = gather_copies(v3, 2, 1, 2)
    start_all(copies3)
    wz = wave(1, 2, az, region, z_peer, 8, total(1, ay, 4, wy))
    arrive_all(copies3)
    coupled = combine(w3m, v3, 512).reshape(4, 8, BLK)
    sums2 = total(1, az, 8, wz)

    def entry(t, where):
        return jnp.sum(jnp.where(where, t, 0.0), axis=1, keepdims=True)

    m0 = entry(sums1, lane == 16 + row128)
    m1 = entry(sums2, lane == 16 + row128)
    m2 = entry(sums2, lane == 20 + row128)
    m3 = entry(sums2, lane == 24) + entry(sums2 * sums2, lane < 16)
    alpha = m0 / m1
    fresh = m0 - 2.0 * alpha * m1 + alpha * alpha * m2
    grow = 1.0 + fresh / m0
    curve = grow * grow * m1 - 2.0 * grow * alpha * m2 + alpha * alpha * m3
    alpha2 = fresh / curve
    ca = alpha + alpha2 * grow
    cb = alpha * alpha2
    ca = jnp.where(low, ca, pltpu.roll(jnp.broadcast_to(ca, (8, BLK)), 4, 0))
    cb = jnp.where(low, cb, pltpu.roll(jnp.broadcast_to(cb, (8, BLK)), 4, 0))
    for k in range(4):
        r0 = twice(v1[local_slot(k)])
        w1 = targets[8 + k]
        w2 = diag[k] + coupled[k] + spread(sums2, k)
        fin[k] = jnp.where(low, ca * r0 - cb * w1, r0 - ca * w1 + cb * w2)
    last = copy(fin.at[pl.ds(2 * (1 - core), 2)], fin_sib, fin_send, fin_recv, sibling)
    last.start()
    last.wait_recv()
    for b in (0, 1):
        mine, theirs = fin[2 * core + b], fin_sib[b]
        left = jnp.where(core == 0, mine, theirs)
        right = jnp.where(core == 0, theirs, mine)
        out_sol[b] = jnp.where(low, left, pltpu.roll(right, 4, 0))
        out_res[b] = jnp.where(low, pltpu.roll(left, 4, 0), right)
    for c in sends + sib_copies + [feat_copy, last]:
        c.wait_send()


def shards(probes, coords, features, noise_var, inv_scale, owner_map, block_pairs):
    vmem = pl.BlockSpec(memory_space=pltpu.VMEM)
    smem = pl.BlockSpec(memory_space=pltpu.SMEM)
    dma = pltpu.SemaphoreType.DMA
    out = jax.ShapeDtypeStruct(probes.shape, F32)
    return pl.pallas_call(
        kernel,
        out_shape=(out, out),
        in_specs=[vmem, vmem, vmem, vmem, smem, smem, smem, vmem, vmem],
        out_specs=(vmem, vmem),
        scratch_shapes=[
            pltpu.VMEM((2, 2, 8, BLK), F32),
            pltpu.VMEM((2, 16, BLK), F32),
            pltpu.VMEM((64, 8, BLK), F32),
            pltpu.VMEM((96, 8, BLK), F32),
            pltpu.VMEM((64, 8, BLK), F32),
            pltpu.VMEM((8, BLK, BLK), BF16),
            pltpu.VMEM((8, BLK, BLK), BF16),
            pltpu.VMEM((BLK, 8), F32),
            pltpu.VMEM((4, 128, BLK), F32),
            pltpu.VMEM((96, 768), F32),
            pltpu.VMEM((32, 512), F32),
            pltpu.VMEM((4, 8, BLK), F32),
            pltpu.VMEM((12, 8, BLK), F32),
            pltpu.VMEM((2, 4, 8, 128), F32),
            pltpu.VMEM((2, 4, 8, 128), F32),
            pltpu.VMEM((2, 8, 8, 128), F32),
            pltpu.VMEM((4, 8, BLK), F32),
            pltpu.VMEM((2, 8, BLK), F32),
            dma((2, 3, 2)), dma((2, 3, 2)),
            dma((3,)), dma((3,)),
            dma((3, 2, 2, 3)), dma((3, 2, 2, 3)),
            dma((2, 3, 7)), dma((2, 3, 7)),
            dma, dma,
        ],
        compiler_params=pltpu.CompilerParams(
            collective_id=0, has_side_effects=True, vmem_limit_bytes=40 << 20
        ),
        name="cg2",
    )(probes, coords, features, noise_var, inv_scale, owner_map, block_pairs, owner_map, block_pairs)


def solution(mesh):
    return jax.shard_map(
        shards,
        mesh=mesh,
        in_specs=(
            P(("region", "dev"), None, None),
            P(("region", "dev"), None, None),
            P(("region", "dev"), None, None),
            P(("region", "dev"), None),
            P(),
            P("region", None),
            P("region", None, None),
        ),
        out_specs=(P(("region", "dev"), None, None), P(("region", "dev"), None, None)),
        check_vma=False,
    )
```

time: 883 us -> 73.6 us (0.08)
  blocking collectives: 775 us -> 0 us
  Pallas kernels: 0 us -> 69.2 us
  matrix products: 38.4 us -> 0 us
  loops' own time: 23.2 us -> 0 us
  local copies, waits for them, and re-layouts: 19.7 us -> 3.48 us
  between operations: 14.8 us -> 0.68 us
    psum x5 -> x0, blocking collectives: 751 us -> none  [the longest x2 320 us: squares_plain(): return lax.psum(column_sum(vectors, vectors), ('region', 'dev'))]
    pallas_call x0 -> x1, Pallas kernels: none -> 69.2 us  [shards(): pl.pallas_call(kernel, out_shape=(out, out), in_specs=[vmem, vmem, vmem,...]
    dot_general x12 -> x0, matrix products: 38.4 us -> none  [the longest x8 37.6 us: apply_tile(): jnp.einsum('ab,cb->ca', kernel_block, vectors, precision=FULL_PRECISION)]
    another operation x4 -> x0, loops' own time: 23.2 us -> none  [the longest x2 23.2 us: shards(): coupled = lax.fori_loop(lower_end, upper_end, visit_entry, zero_sum)]
    all_gather x1 -> x0, blocking collectives: 23.1 us -> none  [shards(): piece_points = lax.all_gather(coords, 'dev', axis=0, tiled=True)]
  transfers between devices with their start and end apart: 2 -> 0, of which waited for: 0 -> 0; matrix products, arithmetic and copies ran while one was open for 4% -> 0% of each run, Pallas kernels for 0% -> 0%
where the time goes in v1:
time: 73.6 us; the launch traced here: 73.4 us
  Pallas kernels  69.2 us (94%)
  local copies, waits for them, and re-layouts  3.48 us (5%)
    pallas_call x1, Pallas kernels, shards(): pl.pallas_call(kernel, out_shape=(out, out), in_specs=[vmem, vmem, vmem,...  69.2 us
    unnamed x16, local copies, waits for them, and re-layouts  3.48 us

profile of v1, /device:TPU:1, one launch (start us, length us, event | category | flops | bytes accessed | tf_op | source)
XLA Modules:
  0.0 73.4 jit_solution(5092867865849662613)
XLA Ops:
  0.6 0.0 copy-start.5
  0.6 0.0 copy-start.1
  0.6 0.7 copy.9.coords
  1.4 0.0 copy-done.5
  1.4 0.0 copy-start.2
  1.4 0.0 copy-start.3
  1.4 0.0 copy-start.4
  1.4 0.1 copy.10.pairs_s.pairs_v
  1.5 0.0 copy-done.1
  1.5 0.6 copy-done.2
  2.1 0.0 copy-done.3
  2.1 0.0 copy-done.4
  2.1 0.0 copy-start
  2.1 0.8 %copy-done = f32[2,16,512]{2,1,0:T(8,128)S(1)} copy-done((f32[2,16,512]{2,1,0:T(8,128)S(1)}, f32[2,16,512]{2,1,0:T(8,128)}, u32[]{:S(2)}) %copy-start) | copy-done | bytes 65560
  2.9 69.2 %cg2.1 = (f32[2,8,512]{2,1,0:T(8,128)S(1)}, f32[2,8,512]{2,1,0:T(8,128)S(1)}) custom-call(f32[2,8,512]{2,1,0:T(8,128)S(1)} %copy-done.1, f32[2,3,512]{2,1,0:T(4,128)S(1)} %copy.9.coords, f32[2,16,512]{2,1,0:T(8,128)S(1)} %copy-done, f32[2,512]{1,0:T(2,128)S(1)} %copy-done.2, f32[3]{0:T(128)S(1)} %copy-done.4, s32[1,64]{1,0:T(1,128)S(1)} %copy-done.3, ...), custom_call_target="tpu_custom_call" | custom-call | tf_op jit(solution)/shard_map/cg2/pallas_call | solution.py:372
  72.1 0.6 copy.14
  72.8 0.6 copy.15
Async XLA Ops:
  0.6 0.7 %copy-start.5 = (s32[1,64,2]{1,2,0:T(2,128)S(1)}, s32[1,64,2]{1,2,0:T(2,128)}, u32[]{:S(2)}) copy-start(s32[1,64,2]{1,2,0:T(2,128)} %param.13) | copy-start | bytes 1540
  0.6 0.9 %copy-start.1 = (f32[2,8,512]{2,1,0:T(8,128)S(1)}, f32[2,8,512]{2,1,0:T(8,128)}, u32[]{:S(2)}) copy-start(f32[2,8,512]{2,1,0:T(8,128)} %probes.1) | copy-start | bytes 98308
  1.4 0.7 copy-start.2
  1.4 0.7 copy-start.3
  1.4 0.7 copy-start.4
  2.1 0.8 %copy-start = (f32[2,16,512]{2,1,0:T(8,128)S(1)}, f32[2,16,512]{2,1,0:T(8,128)}, u32[]{:S(2)}) copy-start(f32[2,16,512]{2,1,0:T(8,128)} %features.1) | copy-start | bytes 196612

commit v2 on v0

v2 whole, which is shorter than its diff:
```python
import jax
import jax.numpy as jnp
from jax import lax
from jax.experimental import pallas as pl
from jax.experimental.pallas import tpu as pltpu
from jax.sharding import PartitionSpec as P

MESH = pl.DeviceIdType.MESH
F32 = jnp.float32
BF16 = jnp.bfloat16
BLK = 512
NT = (((1,), (1,)), ((), ()))
NN = (((1,), (0,)), ((), ()))
PLANE = [(dy, dx) for dy in range(4) for dx in range(4) if dy or dx]


def kernel(
    probes, coords, features, noise, inv_scale, owner_s, pairs_s, owner_v, pairs_v,
    out_sol, out_res,
    points, field, halves, sib_feat, v2, dense, landed, kh, kl, turned, fh, fl, w2f, w2b, diag, targets, packed,
    sib_packed, tile, az1, ap1, az2, ap2,
    pt_send, pt_recv, pf_send, pf_recv, fd_send, fd_recv, sib_send, sib_recv, ag_send, ag_recv,
    rs_send, rs_recv, z1_send, z1_recv, p1_send, p1_recv, z2_send, z2_recv, p2_send, p2_recv,
):
    region = lax.axis_index("region")
    dev = lax.axis_index("dev")
    y, x, core = dev // 8, (dev // 2) % 4, dev % 2
    other = 1 - core
    chip = y * 4 + x
    pos = (chip, x * 4 + y)

    def plane_chip(dy, dx):
        return lax.rem(y + dy, 4) * 4 + lax.rem(x + dx, 4)

    def plane_peer(dy, dx, cc):
        return (region, plane_chip(dy, dx) * 2 + cc)

    def z_peer(d, cc):
        return (lax.rem(region + d, 8), chip * 2 + cc)

    sibling = (region, chip * 2 + other)

    barrier = pltpu.get_barrier_semaphore()
    for dy, dx in PLANE:
        pl.semaphore_signal(barrier, inc=1, device_id=plane_peer(dy, dx, core), device_id_type=MESH)
    for d in range(1, 8):
        pl.semaphore_signal(barrier, inc=1, device_id=z_peer(d, core), device_id_type=MESH)
    pl.semaphore_signal(barrier, inc=1, device_id=sibling, device_id_type=MESH)

    row = lax.broadcasted_iota(jnp.int32, (8, BLK), 0)
    low = row < 4
    lane = lax.broadcasted_iota(jnp.int32, (8, 128), 1)
    row128 = lax.broadcasted_iota(jnp.int32, (8, 128), 0)
    low128 = row128 < 4

    def flip(v):
        return pltpu.roll(v, 4, 0)

    here = core * 16 + chip
    for b in (0, 1):
        for d in range(3):
            points[here, 4 * b + d : 4 * b + d + 1, :] = coords[d, b : b + 1, :]
        points[here, 4 * b + 3 : 4 * b + 4, :] = noise[b : b + 1, :]
    p0, p1 = probes[0], probes[1]
    halves[0] = jnp.where(low, p0, flip(p1))
    halves[1] = jnp.where(low, flip(p0), p1)
    field[chip, core] = halves[core]

    pl.semaphore_wait(barrier, 23)

    sends = []

    def send(src, dst, ssem, rsem, device):
        c = pltpu.make_async_remote_copy(
            src_ref=src, dst_ref=dst, send_sem=ssem, recv_sem=rsem, device_id=device, device_id_type=MESH
        )
        c.start()
        sends.append(c)
        return c

    def arrive(copies):
        for c in copies:
            c.wait_recv()

    sib_field = send(halves.at[other], field.at[chip, core], sib_send.at[0], sib_recv.at[0], sibling)
    point_copies = []
    for n, (dy, dx) in enumerate(PLANE):
        point_copies.append(
            send(points.at[here], points.at[here], pt_send.at[n], pt_recv.at[n], plane_peer(dy, dx, core))
        )
    forwards = [send(points.at[here], points.at[here], pf_send.at[15], pf_recv.at[15], sibling)]
    sib_features = send(features, sib_feat, sib_send.at[1], sib_recv.at[1], sibling)

    sx, sy, st = inv_scale[0], inv_scale[1], inv_scale[2]

    def make_tile(index, left, right):
        turned[...] = jnp.transpose(left)
        rx, ry, rt = right[0:1, :] * sx, right[1:2, :] * sy, right[2:3, :] * st

        def rows(i, _):
            span = pl.ds(pl.multiple_of(i * 16, 16), 16)
            part = turned[span, :]
            dx = part[:, 0:1] * sx - rx
            dy = part[:, 1:2] * sy - ry
            dt = part[:, 2:3] * st - rt
            sq = jnp.maximum(dx * dx + dy * dy, 1e-30)
            a = jnp.maximum(1.0 - sq * lax.rsqrt(sq), 0.0)
            b = jnp.maximum(1.0 - jnp.abs(dt), 0.0)
            m = a * b
            m = m * m
            m = m * m
            value = m * ((1.25 - a) * (1.25 - b))
            high = value.astype(BF16)
            kh[index, span, :] = high
            kl[index, span, :] = (value - high.astype(F32)).astype(BF16)
            return 0

        lax.fori_loop(0, 32, rows, 0, unroll=4)

    def points_of(index, b):
        v = points[index]
        if isinstance(b, int):
            return v if b == 0 else flip(v)
        return jnp.where(b == 0, v, flip(v))

    def field_of(q, c, b):
        v = field[q, c]
        f = flip(v)
        first, second = jnp.where(low, v, f), jnp.where(low, f, v)
        if isinstance(b, int):
            return first if b == 0 else second
        return jnp.where(b == 0, first, second)

    def split(v):
        high = v.astype(BF16).astype(F32)
        return jnp.where(low, high, v - high).astype(BF16)

    def fold(v, high, rest, dims):
        s = lax.dot_general(v, high, dims, preferred_element_type=F32)
        s = s + lax.dot_general(v, rest, dims, preferred_element_type=F32)
        return s + flip(s)

    def apply(v, index, dims):
        return 4.0 * fold(v, kh[index], kl[index], dims)

    mine0 = points[here]
    make_tile(2 * core, mine0, mine0)

    sib_field.wait_recv()
    field_copies = []
    for n, (dy, dx) in enumerate(PLANE):
        field_copies.append(
            send(field.at[chip], field.at[chip], fd_send.at[n], fd_recv.at[n], plane_peer(dy, dx, core))
        )

    sib_features.wait_recv()

    def feature_block(k):
        return jnp.where(core == k // 2, features[k % 2], sib_feat[k % 2])

    for k in range(4):
        f = feature_block(k)
        high = f.astype(BF16)
        fh[k] = high
        fl[k] = (f - high.astype(F32)).astype(BF16)

    def loads(values):
        t = None
        for k in range(4):
            s = fold(split(values(k)), fh[k], fl[k], NT)
            t = s if t is None else t + s
        tile[:, 0:16] = t
        return tile[...]

    tile[...] = jnp.zeros_like(tile)
    az1[region] = loads(lambda k: field_of(chip, k // 2, k % 2))
    z1 = []
    for d in range(1, 8):
        z1.append(send(az1.at[region], az1.at[region], z1_send.at[d - 1], z1_recv.at[d - 1], z_peer(d, core)))

    lane64 = lax.broadcasted_iota(jnp.int32, (64, 64), 1)
    owner_row = owner_v[...].astype(F32)
    ids = jnp.transpose(pairs_v[0].astype(F32)).astype(jnp.int32)
    slot_a = jnp.sum(jnp.where(ids[:, 0:1] == lane64, owner_row, 0.0), axis=1, keepdims=True)
    slot_b = jnp.sum(jnp.where(ids[:, 1:2] == lane64, owner_row, 0.0), axis=1, keepdims=True)
    first, second = [], []
    for i in range(4):
        first.append(owner_s[0, pairs_s[0, 0, chip * 4 + i]])
        second.append(owner_s[0, pairs_s[0, 1, chip * 4 + i]])

    j = lax.broadcasted_iota(jnp.int32, (1, 768), 1)
    n = j >> 3
    side = (j >> 2) & 1
    h = (n >= 48).astype(jnp.int32)
    rest = n - h * 48
    place = (rest * 171) >> 9
    e = rest - place * 3
    q = jnp.where(h == 0, place, (place & 3) * 4 + (place >> 2))
    pick = lax.broadcasted_iota(jnp.int32, (64, 768), 0) == q * 4 + h * 2 + e
    listed = jnp.sum(jnp.where(pick, jnp.where(side == 0, slot_a, slot_b), 0.0), axis=0, keepdims=True)
    lanes2 = jnp.where(e == 2, (q * 4 + side * 2 + h).astype(F32), listed)
    same_column = (lax.broadcasted_iota(jnp.int32, (8, 768), 0) & 3) == (j & 3)
    wanted = []
    for i in range(4):
        wanted += [first[i], second[i]]
    for k in range(4):
        wanted.append(chip * 4 + k)
    for k in range(12):
        hit = (lanes2 == wanted[k].astype(F32)) & same_column
        w2f[8 * k : 8 * k + 8, :] = jnp.where(hit, 1.0, 0.0)
    w2b[...] = w2f[...].astype(BF16)
    factor = []
    for k in range(4):
        me = wanted[8 + k].astype(F32)
        count = jnp.where(slot_a == me, 1.0, 0.0) + jnp.where(slot_b == me, 1.0, 0.0)
        factor.append(1.0 + jnp.sum(count, axis=0, keepdims=True))
    lane32 = lax.broadcasted_iota(jnp.int32, (256, 32), 1)
    slot32 = jnp.zeros((256, 32), jnp.int32)
    for i in range(8):
        slot32 = jnp.where((lane32 >> 2) == i, wanted[i], slot32)
    row32 = lax.broadcasted_iota(jnp.int32, (256, 32), 0)
    w3 = jnp.where((slot32 == (row32 >> 2)) & ((lane32 & 3) == (row32 & 3)), 1.0, 0.0).astype(BF16)

    mine1 = flip(points[here])
    make_tile(2 * core + 1, mine1, mine1)

    for n, (dy, dx) in enumerate(PLANE):
        back = core * 16 + plane_chip(-dy % 4, -dx % 4)
        point_copies[n].wait_recv()
        forwards.append(send(points.at[back], points.at[back], pf_send.at[n], pf_recv.at[n], sibling))

    arrive(z1)
    t = az1[0]
    for i in range(1, 8):
        t = t + az1[i]
    ap1[chip] = t
    a1 = []
    for n, (dy, dx) in enumerate(PLANE):
        a1.append(send(ap1.at[chip], ap1.at[chip], p1_send.at[n], p1_recv.at[n], plane_peer(dy, dx, core)))

    arrive(forwards)
    for b in (0, 1):
        theirs = points_of(other * 16 + chip, b)
        make_tile(2 * other + b, theirs, theirs)

    def where_is(s):
        return s >> 2, (s >> 1) & 1, s & 1

    for i in range(4):
        qa, ca, ba = where_is(first[i])
        qb, cb, bb = where_is(second[i])
        make_tile(4 + i, points_of(ca * 16 + qa, ba), points_of(cb * 16 + qb, bb))

    def noise_of(k):
        return points[(k // 2) * 16 + chip, 4 * (k % 2) + 3 : 4 * (k % 2) + 4, :]

    for k in range(4):
        mine = field_of(chip, k // 2, k % 2)
        diag[k] = factor[k] * apply(split(mine), k, NN) + noise_of(k) * mine

    arrive(field_copies)
    for i in range(4):
        va, vb = field_of(*where_is(first[i])), field_of(*where_is(second[i]))
        ya = apply(split(vb), 4 + i, NT)
        yb = apply(split(va), 4 + i, NN)
        v2[(i // 2) * 48 + pos[i // 2] * 3 + i % 2] = jnp.where(low, ya, yb)

    arrive(a1)
    g1 = ap1[0]
    for i in range(1, 16):
        g1 = g1 + ap1[i]

    def spread(g, k):
        f = feature_block(k)
        acc = g[:, 0:1] * f[0:1, :]
        for i in range(1, 16):
            acc = acc + g[:, i : i + 1] * f[i : i + 1, :]
        return acc

    def gather_stage(stage_index):
        out = []
        for h in (0, 1):
            if stage_index == 0:
                span = pl.ds(h * 48 + pos[h] * 3, 3)
                steps = [(0, d) if h == 0 else (d, 0) for d in (1, 2, 3)]
            else:
                span = pl.ds(h * 48 + (y, x)[h] * 12, 12)
                steps = [(d, 0) if h == 0 else (0, d) for d in (1, 2, 3)]
            for d, (dy, dx) in enumerate(steps):
                sem = (stage_index, h, d)
                out.append(send(v2.at[span], v2.at[span], ag_send.at[sem], ag_recv.at[sem], plane_peer(dy, dx, core)))
        return out

    for b in (0, 1):
        d0 = diag[b] + spread(g1, b)
        d1 = diag[2 + b] + spread(g1, 2 + b)
        v2[b * 48 + pos[b] * 3 + 2] = jnp.where(low, d0, d1)
    arrive(gather_stage(0))
    arrive(gather_stage(1))

    acc = None
    for lo_row in range(0, 768, 256):
        part = v2[lo_row // 8 : lo_row // 8 + 32].reshape(256, BLK)
        w = w2b[:, lo_row : lo_row + 256]
        high = part.astype(BF16)
        less = (part - high.astype(F32)).astype(BF16)
        s = lax.dot_general(w, high, NN, preferred_element_type=F32)
        s = s + lax.dot_general(w, less, NN, preferred_element_type=F32)
        acc = s if acc is None else acc + s
    targets[...] = acc.reshape(12, 8, BLK)

    form = jnp.zeros((8, BLK), F32)
    for i in range(4):
        wa = targets[2 * i]
        ya = apply(split(targets[2 * i + 1]), 4 + i, NT)
        dense[i, 0] = ya
        form = form + 2.0 * (wa * ya)
    dot00, dot01, dot11 = jnp.zeros((8, BLK), F32), jnp.zeros((8, BLK), F32), jnp.zeros((8, BLK), F32)
    for k in range(4):
        w1 = targets[8 + k]
        r0 = field_of(chip, k // 2, k % 2)
        z = factor[k] * apply(split(w1), k, NN) + noise_of(k) * w1
        packed[k] = jnp.where(low, w1, z)
        form = form + w1 * z
        dot00 = dot00 + r0 * r0
        dot01 = dot01 + r0 * w1
        dot11 = dot11 + w1 * w1
    g2 = loads(lambda k: targets[8 + k])
    stat_a = jnp.sum(jnp.where(low, dot01, dot11), axis=1, keepdims=True)
    stat_b = jnp.sum(jnp.where(low, form, dot00), axis=1, keepdims=True)
    stats = jnp.where((lane < 16) & ((row128 >> 2) == core), g2, 0.0)
    stats = jnp.where(lane == 16 + 2 * core, stat_a, stats)
    stats = jnp.where(lane == 17 + 2 * core, stat_b, stats)
    az2[core, region] = stats
    z2 = [send(az2.at[core, region], az2.at[core, region], z2_send.at[7, 0], z2_recv.at[7, 0], sibling)]
    for d in range(1, 8):
        for cc in (0, 1):
            z2.append(
                send(
                    az2.at[core, region], az2.at[core, region], z2_send.at[d - 1, cc], z2_recv.at[d - 1, core],
                    z_peer(d, cc),
                )
            )
    sib_pack = send(packed.at[pl.ds(2 * other, 2)], sib_packed, sib_send.at[2], sib_recv.at[2], sibling)

    results = []
    for i in range(4):
        yb = apply(split(targets[2 * i]), 4 + i, NN)
        results.append(jnp.where(low, dense[i, 0], yb))
    results = jnp.concatenate(results, axis=0)
    high = results.astype(BF16)
    less = (results - high.astype(F32)).astype(BF16)
    s = lax.dot_general(w3, high, NN, preferred_element_type=F32)
    s = s + lax.dot_general(w3, less, NN, preferred_element_type=F32)
    dense[...] = s.reshape(16, 2, 8, BLK)
    landed[here] = dense[chip, core]
    send(dense.at[chip, other], landed.at[here], rs_send.at[15, 0], rs_recv.at[15, 0], sibling)
    for n, (dy, dx) in enumerate(PLANE):
        for cc in (0, 1):
            send(
                dense.at[plane_chip(dy, dx), cc], landed.at[here], rs_send.at[n, cc], rs_recv.at[n, core],
                plane_peer(dy, dx, cc),
            )

    def waiting(dst, ssem, rsem):
        return pltpu.make_async_remote_copy(
            src_ref=dst, dst_ref=dst, send_sem=ssem, recv_sem=rsem, device_id=sibling, device_id_type=MESH
        )

    z2[0].wait_recv()
    for d in range(1, 8):
        for cc in (0, 1):
            waiting(
                az2.at[cc, lax.rem(region + 8 - d, 8)], z2_send.at[d - 1, cc], z2_recv.at[d - 1, cc]
            ).wait_recv()
    t = az2[0, 0]
    for i in range(1, 16):
        t = t + az2[i // 8, i % 8]
    ap2[chip] = t
    a2 = []
    for n, (dy, dx) in enumerate(PLANE):
        a2.append(send(ap2.at[chip], ap2.at[chip], p2_send.at[n], p2_recv.at[n], plane_peer(dy, dx, core)))

    sib_pack.wait_recv()
    waiting(landed.at[other * 16 + chip], rs_send.at[15, 0], rs_recv.at[15, 0]).wait_recv()
    for n, (dy, dx) in enumerate(PLANE):
        for cc in (0, 1):
            waiting(
                landed.at[cc * 16 + plane_chip(-dy % 4, -dx % 4)], rs_send.at[n, cc], rs_recv.at[n, cc]
            ).wait_recv()
    total = []
    for cc in (0, 1):
        s = landed[cc * 16]
        for i in range(1, 16):
            s = s + landed[cc * 16 + i]
        total.append(s)
    w1s, w2s = [], []
    for b in (0, 1):
        mine, theirs = packed[2 * core + b], sib_packed[b]
        c0 = jnp.where(core == 0, mine, theirs)
        c1 = jnp.where(core == 0, theirs, mine)
        w1s.append(jnp.where(low, c0, flip(c1)))
        z = jnp.where(low, flip(c0), c1)
        pair = jnp.where(low, total[0], flip(total[1])) if b == 0 else jnp.where(low, flip(total[0]), total[1])
        w2s.append(z + pair)

    arrive(a2)
    t = ap2[0]
    for i in range(1, 16):
        t = t + ap2[i]
    a0, b0 = jnp.broadcast_to(t[:, 16:17], (8, 128)), jnp.broadcast_to(t[:, 17:18], (8, 128))
    a1, b1 = jnp.broadcast_to(t[:, 18:19], (8, 128)), jnp.broadcast_to(t[:, 19:20], (8, 128))
    squares = jnp.sum(jnp.where(lane < 16, t * t, 0.0), axis=1, keepdims=True)
    m1 = jnp.where(low128, a0, flip(a1))
    m2 = jnp.where(low128, flip(a0), a1)
    m3 = jnp.where(low128, b0, flip(b1)) + squares
    m0 = jnp.where(low128, flip(b0), b1)
    alpha = m0 / m1
    fresh = m0 - 2.0 * alpha * m1 + alpha * alpha * m2
    grow = 1.0 + fresh / m0
    curve = grow * grow * m1 - 2.0 * grow * alpha * m2 + alpha * alpha * m3
    alpha2 = fresh / curve
    ca = (alpha + alpha2 * grow)[:, 0:1]
    cb = (alpha * alpha2)[:, 0:1]
    for b in (0, 1):
        r0, w1 = probes[b], w1s[b]
        f = features[b]
        w2 = w2s[b]
        for i in range(16):
            w2 = w2 + t[:, i : i + 1] * f[i : i + 1, :]
        out_sol[b] = ca * r0 - cb * w1
        out_res[b] = r0 - ca * w1 + cb * w2
    for c in sends:
        c.wait_send()


def shards(probes, coords, features, noise_var, inv_scale, owner_map, block_pairs):
    vmem = pl.BlockSpec(memory_space=pltpu.VMEM)
    smem = pl.BlockSpec(memory_space=pltpu.SMEM)
    dma = pltpu.SemaphoreType.DMA
    out = jax.ShapeDtypeStruct(probes.shape, F32)
    coords = jnp.transpose(coords, (1, 0, 2))
    block_pairs = jnp.transpose(block_pairs, (0, 2, 1))
    pairs_of = []
    for shape in ((15,), (16,), (15,), (3,), (2, 2, 3), (16, 2), (7,), (15,), (8, 2), (15,)):
        pairs_of += [dma(shape), dma(shape)]
    return pl.pallas_call(
        kernel,
        out_shape=(out, out),
        in_specs=[vmem, vmem, vmem, vmem, smem, smem, smem, vmem, vmem],
        out_specs=(vmem, vmem),
        scratch_shapes=[
            pltpu.VMEM((32, 8, BLK), F32),
            pltpu.VMEM((16, 2, 8, BLK), F32),
            pltpu.VMEM((2, 8, BLK), F32),
            pltpu.VMEM((2, 16, BLK), F32),
            pltpu.VMEM((96, 8, BLK), F32),
            pltpu.VMEM((16, 2, 8, BLK), F32),
            pltpu.VMEM((32, 8, BLK), F32),
            pltpu.VMEM((8, BLK, BLK), BF16),
            pltpu.VMEM((8, BLK, BLK), BF16),
            pltpu.VMEM((BLK, 8), F32),
            pltpu.VMEM((4, 16, BLK), BF16),
            pltpu.VMEM((4, 16, BLK), BF16),
            pltpu.VMEM((96, 768), F32),
            pltpu.VMEM((96, 768), BF16),
            pltpu.VMEM((4, 8, BLK), F32),
            pltpu.VMEM((12, 8, BLK), F32),
            pltpu.VMEM((4, 8, BLK), F32),
            pltpu.VMEM((2, 8, BLK), F32),
            pltpu.VMEM((8, 128), F32),
            pltpu.VMEM((8, 8, 128), F32),
            pltpu.VMEM((16, 8, 128), F32),
            pltpu.VMEM((2, 8, 8, 128), F32),
            pltpu.VMEM((16, 8, 128), F32),
        ]
        + pairs_of,
        compiler_params=pltpu.CompilerParams(
            collective_id=0, has_side_effects=True, vmem_limit_bytes=40 << 20
        ),
        name="cg2",
    )(probes, coords, features, noise_var, inv_scale, owner_map, block_pairs, owner_map, block_pairs)


def solution(mesh):
    return jax.shard_map(
        shards,
        mesh=mesh,
        in_specs=(
            P(("region", "dev"), None, None),
            P(("region", "dev"), None, None),
            P(("region", "dev"), None, None),
            P(("region", "dev"), None),
            P(),
            P("region", None),
            P("region", None, None),
        ),
        out_specs=(P(("region", "dev"), None, None), P(("region", "dev"), None, None)),
        check_vma=False,
    )
```

time: 883 us -> 67.5 us (0.08)
  blocking collectives: 775 us -> 0 us
  Pallas kernels: 0 us -> 61.7 us
  matrix products: 38.4 us -> 0 us
  loops' own time: 23.2 us -> 0 us
  local copies, waits for them, and re-layouts: 19.7 us -> 4.89 us
  between operations: 14.8 us -> 0.67 us
    psum x5 -> x0, blocking collectives: 751 us -> none  [the longest x2 320 us: squares_plain(): return lax.psum(column_sum(vectors, vectors), ('region', 'dev'))]
    pallas_call x0 -> x1, Pallas kernels: none -> 61.7 us  [shards(): pl.pallas_call(kernel, out_shape=(out, out), in_specs=[vmem, vmem, vmem,...]
    dot_general x12 -> x0, matrix products: 38.4 us -> none  [the longest x8 37.6 us: apply_tile(): jnp.einsum('ab,cb->ca', kernel_block, vectors, precision=FULL_PRECISION)]
    another operation x4 -> x0, loops' own time: 23.2 us -> none  [the longest x2 23.2 us: shards(): coupled = lax.fori_loop(lower_end, upper_end, visit_entry, zero_sum)]
    all_gather x1 -> x0, blocking collectives: 23.1 us -> none  [shards(): piece_points = lax.all_gather(coords, 'dev', axis=0, tiled=True)]
  transfers between devices with their start and end apart: 2 -> 0, of which waited for: 0 -> 0; matrix products, arithmetic and copies ran while one was open for 4% -> 0% of each run, Pallas kernels for 0% -> 0%
where the time goes in v2:
time: 67.5 us; the launch traced here: 67.2 us
  Pallas kernels  61.7 us (91%)
  local copies, waits for them, and re-layouts  4.89 us (7%)
    pallas_call x1, Pallas kernels, shards(): pl.pallas_call(kernel, out_shape=(out, out), in_specs=[vmem, vmem, vmem,...  61.7 us
    unnamed x16, local copies, waits for them, and re-layouts  4.89 us

profile of v2, /device:TPU:1, one launch (start us, length us, event | category | flops | bytes accessed | tf_op | source)
XLA Modules:
  0.0 67.2 jit_solution(3208386850005206967)
XLA Ops:
  0.6 0.0 copy-start.6
  0.6 0.0 copy-start.4
  0.7 0.0 copy-start.5
  0.7 0.6 copy-done.6
  1.3 0.0 copy-done.4
  1.3 0.0 copy-done.5
  1.3 0.0 copy-start
  1.3 0.8 %copy-done = f32[2,16,512]{2,1,0:T(8,128)S(1)} copy-done((f32[2,16,512]{2,1,0:T(8,128)S(1)}, f32[2,16,512]{2,1,0:T(8,128)}, u32[]{:S(2)}) %copy-start) | copy-done | bytes 65560
  2.2 0.0 copy-start.1
  2.2 0.8 %copy-done.1 = f32[2,8,512]{2,1,0:T(8,128)S(1)} copy-done((f32[2,8,512]{2,1,0:T(8,128)S(1)}, f32[2,8,512]{2,1,0:T(8,128)}, u32[]{:S(2)}) %copy-start.1) | copy-done | bytes 32792
  2.9 0.0 copy-start.2
  2.9 0.7 %copy-done.2 = f32[2,3,512]{2,0,1:T(2,128)S(1)} copy-done((f32[2,3,512]{2,0,1:T(2,128)S(1)}, f32[2,3,512]{2,0,1:T(2,128)}, u32[]{:S(2)}) %copy-start.2) | copy-done | bytes 12312
  3.6 0.0 copy-start.3
  3.6 0.7 %copy-done.3 = f32[2,512]{1,0:T(2,128)S(1)} copy-done((f32[2,512]{1,0:T(2,128)S(1)}, f32[2,512]{1,0:T(2,128)}, u32[]{:S(2)}) %copy-start.3) | copy-done | bytes 4120
  4.3 61.7 %cg2.1 = (f32[2,8,512]{2,1,0:T(8,128)S(1)}, f32[2,8,512]{2,1,0:T(8,128)S(1)}) custom-call(f32[2,8,512]{2,1,0:T(8,128)S(1)} %copy-done.1, f32[3,2,512]{2,1,0:T(2,128)S(1)} %bitcast.2, f32[2,16,512]{2,1,0:T(8,128)S(1)} %copy-done, f32[2,512]{1,0:T(2,128)S(1)} %copy-done.3, f32[3]{0:T(128)S(1)} %copy-done.6, s32[1,64]{1,0:T(1,128)S(1)} %copy-done.5, ...), custom_call_target="tpu_custom_call" | custom-call | tf_op jit(solution)/shard_map/cg2/pallas_call | solution.py:447
  66.0 0.6 copy.11
  66.6 0.6 copy.12
Async XLA Ops:
  0.6 0.7 copy-start.6
  0.6 0.7 %copy-start.4 = (s32[1,64,2]{1,2,0:T(2,128)S(1)}, s32[1,64,2]{1,2,0:T(2,128)}, u32[]{:S(2)}) copy-start(s32[1,64,2]{1,2,0:T(2,128)} %param.13) | copy-start | bytes 1540
  0.7 0.7 %copy-start.5 = (s32[1,64]{1,0:T(1,128)S(1)}, s32[1,64]{1,0:T(1,128)}, u32[]{:S(2)}) copy-start(s32[1,64]{1,0:T(1,128)} %owner_v.1) | copy-start | bytes 772
  1.3 0.8 %copy-start = (f32[2,16,512]{2,1,0:T(8,128)S(1)}, f32[2,16,512]{2,1,0:T(8,128)}, u32[]{:S(2)}) copy-start(f32[2,16,512]{2,1,0:T(8,128)} %features.1) | copy-start | bytes 196612
  2.2 0.8 %copy-start.1 = (f32[2,8,512]{2,1,0:T(8,128)S(1)}, f32[2,8,512]{2,1,0:T(8,128)}, u32[]{:S(2)}) copy-start(f32[2,8,512]{2,1,0:T(8,128)} %probes.1) | copy-start | bytes 98308
  2.9 0.7 %copy-start.2 = (f32[2,3,512]{2,0,1:T(2,128)S(1)}, f32[2,3,512]{2,0,1:T(2,128)}, u32[]{:S(2)}) copy-start(f32[2,3,512]{2,0,1:T(2,128)} %param.8) | copy-start | bytes 36868
  3.6 0.7 %copy-start.3 = (f32[2,512]{1,0:T(2,128)S(1)}, f32[2,512]{1,0:T(2,128)}, u32[]{:S(2)}) copy-start(f32[2,512]{1,0:T(2,128)} %noise.1) | copy-start | bytes 12292

commit v3 on v2

--- a/solution.py
+++ b/solution.py
@@ -15,10 +15,11 @@
 
 
 def kernel(
-    probes, coords, features, noise, inv_scale, owner_s, pairs_s, owner_v, pairs_v,
-    out_sol, out_res,
-    points, field, halves, sib_feat, v2, dense, landed, kh, kl, turned, fh, fl, w2f, w2b, diag, targets, packed,
-    sib_packed, tile, az1, ap1, az2, ap2,
+    probes_in, coords_in, features_in, noise_in, inv_scale_in, owner_in, pairs_in,
+    out,
+    probes, coords, features, noise, inv_scale, owner_s, pairs_s, owner_v, pairs_v, in_sem,
+    points, field, halves, cross, sib_cross, v2, dense, landed, kh, kl, turned, fh, fl, w2f, w2b, diag, targets,
+    tile, az1, ac1, ap1, az2, ap2,
     pt_send, pt_recv, pf_send, pf_recv, fd_send, fd_recv, sib_send, sib_recv, ag_send, ag_recv,
     rs_send, rs_recv, z1_send, z1_recv, p1_send, p1_recv, z2_send, z2_recv, p2_send, p2_recv,
 ):
@@ -40,6 +41,15 @@
 
     sibling = (region, chip * 2 + other)
 
+    loads_in = []
+    for src, dst in (
+        (coords_in, coords), (noise_in, noise), (probes_in, probes), (features_in, features), (inv_scale_in, inv_scale),
+        (owner_in, owner_v), (pairs_in, pairs_v), (owner_in, owner_s), (pairs_in, pairs_s),
+    ):
+        c = pltpu.make_async_copy(src, dst, in_sem.at[len(loads_in)])
+        c.start()
+        loads_in.append(c)
+
     barrier = pltpu.get_barrier_semaphore()
     for dy, dx in PLANE:
         pl.semaphore_signal(barrier, inc=1, device_id=plane_peer(dy, dx, core), device_id_type=MESH)
@@ -56,6 +66,8 @@
     def flip(v):
         return pltpu.roll(v, 4, 0)
 
+    for c in loads_in:
+        c.wait()
     here = core * 16 + chip
     for b in (0, 1):
         for d in range(3):
@@ -89,7 +101,6 @@
             send(points.at[here], points.at[here], pt_send.at[n], pt_recv.at[n], plane_peer(dy, dx, core))
         )
     forwards = [send(points.at[here], points.at[here], pf_send.at[15], pf_recv.at[15], sibling)]
-    sib_features = send(features, sib_feat, sib_send.at[1], sib_recv.at[1], sibling)
 
     sx, sy, st = inv_scale[0], inv_scale[1], inv_scale[2]
 
@@ -115,7 +126,7 @@
             kl[index, span, :] = (value - high.astype(F32)).astype(BF16)
             return 0
 
-        lax.fori_loop(0, 32, rows, 0, unroll=4)
+        lax.fori_loop(0, 32, rows, 0, unroll=32)
 
     def points_of(index, b):
         v = points[index]
@@ -143,8 +154,31 @@
     def apply(v, index, dims):
         return 4.0 * fold(v, kh[index], kl[index], dims)
 
-    mine0 = points[here]
-    make_tile(2 * core, mine0, mine0)
+    for b in (0, 1):
+        f = features[b]
+        high = f.astype(BF16)
+        fh[b] = high
+        fl[b] = (f - high.astype(F32)).astype(BF16)
+
+    def stack(v):
+        top = v.astype(BF16).astype(F32)
+        return jnp.concatenate([top, v - top], axis=0).astype(BF16)
+
+    def unstack(v, high, rest, dims):
+        d = lax.dot_general(v, high, dims, preferred_element_type=F32)
+        d = d + lax.dot_general(v, rest, dims, preferred_element_type=F32)
+        return d[0:8] + d[8:16]
+
+    def loads(v0, v1):
+        tile[:, 0:16] = unstack(v0, fh[0], fl[0], NT) + unstack(v1, fh[1], fl[1], NT)
+        return tile[...]
+
+    tile[...] = jnp.zeros_like(tile)
+    first_stack = [stack(probes[b]) for b in (0, 1)]
+    az1[region] = loads(*first_stack)
+    z1 = []
+    for d in range(1, 8):
+        z1.append(send(az1.at[region], az1.at[region], z1_send.at[d - 1], z1_recv.at[d - 1], z_peer(d, core)))
 
     sib_field.wait_recv()
     field_copies = []
@@ -153,30 +187,10 @@
             send(field.at[chip], field.at[chip], fd_send.at[n], fd_recv.at[n], plane_peer(dy, dx, core))
         )
 
-    sib_features.wait_recv()
-
-    def feature_block(k):
-        return jnp.where(core == k // 2, features[k % 2], sib_feat[k % 2])
-
-    for k in range(4):
-        f = feature_block(k)
-        high = f.astype(BF16)
-        fh[k] = high
-        fl[k] = (f - high.astype(F32)).astype(BF16)
-
-    def loads(values):
-        t = None
-        for k in range(4):
-            s = fold(split(values(k)), fh[k], fl[k], NT)
-            t = s if t is None else t + s
-        tile[:, 0:16] = t
-        return tile[...]
-
-    tile[...] = jnp.zeros_like(tile)
-    az1[region] = loads(lambda k: field_of(chip, k // 2, k % 2))
-    z1 = []
-    for d in range(1, 8):
-        z1.append(send(az1.at[region], az1.at[region], z1_send.at[d - 1], z1_recv.at[d - 1], z_peer(d, core)))
+    mine0 = points[here]
+    make_tile(0, mine0, mine0)
+    mine1 = flip(mine0)
+    make_tile(1, mine1, mine1)
 
     lane64 = lax.broadcasted_iota(jnp.int32, (64, 64), 1)
     owner_row = owner_v[...].astype(F32)
@@ -203,15 +217,17 @@
     wanted = []
     for i in range(4):
         wanted += [first[i], second[i]]
-    for k in range(4):
-        wanted.append(chip * 4 + k)
-    for k in range(12):
+    for k in range(8):
         hit = (lanes2 == wanted[k].astype(F32)) & same_column
         w2f[8 * k : 8 * k + 8, :] = jnp.where(hit, 1.0, 0.0)
+    block_of_row = lax.broadcasted_iota(jnp.int32, (8, 768), 0) >> 2
+    for k in (0, 1):
+        hit = (lanes2 == (chip * 4 + 2 * k + block_of_row).astype(F32)) & same_column
+        w2f[64 + 8 * k : 72 + 8 * k, :] = jnp.where(hit, 1.0, 0.0)
     w2b[...] = w2f[...].astype(BF16)
     factor = []
-    for k in range(4):
-        me = wanted[8 + k].astype(F32)
+    for b in (0, 1):
+        me = (dev * 2 + b).astype(F32)
         count = jnp.where(slot_a == me, 1.0, 0.0) + jnp.where(slot_b == me, 1.0, 0.0)
         factor.append(1.0 + jnp.sum(count, axis=0, keepdims=True))
     lane32 = lax.broadcasted_iota(jnp.int32, (256, 32), 1)
@@ -221,27 +237,27 @@
     row32 = lax.broadcasted_iota(jnp.int32, (256, 32), 0)
     w3 = jnp.where((slot32 == (row32 >> 2)) & ((lane32 & 3) == (row32 & 3)), 1.0, 0.0).astype(BF16)
 
-    mine1 = flip(points[here])
-    make_tile(2 * core + 1, mine1, mine1)
-
-    for n, (dy, dx) in enumerate(PLANE):
-        back = core * 16 + plane_chip(-dy % 4, -dx % 4)
-        point_copies[n].wait_recv()
-        forwards.append(send(points.at[back], points.at[back], pf_send.at[n], pf_recv.at[n], sibling))
-
     arrive(z1)
     t = az1[0]
     for i in range(1, 8):
         t = t + az1[i]
-    ap1[chip] = t
+    ac1[0] = t
+    sib_loads = send(ac1.at[0], ac1.at[1], sib_send.at[3], sib_recv.at[3], sibling)
+    for n, (dy, dx) in enumerate(PLANE):
+        back = core * 16 + plane_chip(-dy % 4, -dx % 4)
+        point_copies[n].wait_recv()
+        forwards.append(send(points.at[back], points.at[back], pf_send.at[n], pf_recv.at[n], sibling))
+
+    sib_loads.wait_recv()
+    ap1[chip] = ac1[0] + ac1[1]
     a1 = []
     for n, (dy, dx) in enumerate(PLANE):
         a1.append(send(ap1.at[chip], ap1.at[chip], p1_send.at[n], p1_recv.at[n], plane_peer(dy, dx, core)))
 
+    for b in (0, 1):
+        diag[b] = factor[b] * (4.0 * unstack(first_stack[b], kh[b], kl[b], NN)) + noise[b : b + 1, :] * probes[b]
+
     arrive(forwards)
-    for b in (0, 1):
-        theirs = points_of(other * 16 + chip, b)
-        make_tile(2 * other + b, theirs, theirs)
 
     def where_is(s):
         return s >> 2, (s >> 1) & 1, s & 1
@@ -249,33 +265,30 @@
     for i in range(4):
         qa, ca, ba = where_is(first[i])
         qb, cb, bb = where_is(second[i])
-        make_tile(4 + i, points_of(ca * 16 + qa, ba), points_of(cb * 16 + qb, bb))
-
-    def noise_of(k):
-        return points[(k // 2) * 16 + chip, 4 * (k % 2) + 3 : 4 * (k % 2) + 4, :]
-
-    for k in range(4):
-        mine = field_of(chip, k // 2, k % 2)
-        diag[k] = factor[k] * apply(split(mine), k, NN) + noise_of(k) * mine
-
-    arrive(field_copies)
-    for i in range(4):
-        va, vb = field_of(*where_is(first[i])), field_of(*where_is(second[i]))
-        ya = apply(split(vb), 4 + i, NT)
-        yb = apply(split(va), 4 + i, NN)
-        v2[(i // 2) * 48 + pos[i // 2] * 3 + i % 2] = jnp.where(low, ya, yb)
+        make_tile(2 + i, points_of(ca * 16 + qa, ba), points_of(cb * 16 + qb, bb))
 
     arrive(a1)
     g1 = ap1[0]
     for i in range(1, 16):
         g1 = g1 + ap1[i]
 
-    def spread(g, k):
-        f = feature_block(k)
-        acc = g[:, 0:1] * f[0:1, :]
-        for i in range(1, 16):
+    def spread(g, f, acc):
+        for i in range(16):
             acc = acc + g[:, i : i + 1] * f[i : i + 1, :]
         return acc
+
+    d0 = spread(g1, features[0], diag[0])
+    d1 = spread(g1, features[1], diag[1])
+    cross[0] = jnp.where(low, d0, flip(d1))
+    cross[1] = jnp.where(low, flip(d0), d1)
+    sib_diag = send(cross.at[other], sib_cross.at[0], sib_send.at[1], sib_recv.at[1], sibling)
+
+    arrive(field_copies)
+    for i in range(4):
+        va, vb = field_of(*where_is(first[i])), field_of(*where_is(second[i]))
+        ya = apply(split(vb), 2 + i, NT)
+        yb = apply(split(va), 2 + i, NN)
+        v2[(i // 2) * 48 + pos[i // 2] * 3 + i % 2] = jnp.where(low, ya, yb)
 
     def gather_stage(stage_index):
         out = []
@@ -291,10 +304,12 @@
                 out.append(send(v2.at[span], v2.at[span], ag_send.at[sem], ag_recv.at[sem], plane_peer(dy, dx, core)))
         return out
 
-    for b in (0, 1):
-        d0 = diag[b] + spread(g1, b)
-        d1 = diag[2 + b] + spread(g1, 2 + b)
-        v2[b * 48 + pos[b] * 3 + 2] = jnp.where(low, d0, d1)
+    sib_diag.wait_recv()
+    mine, theirs = cross[core], sib_cross[0]
+    c0 = jnp.where(core == 0, mine, theirs)
+    c1 = jnp.where(core == 0, theirs, mine)
+    v2[pos[0] * 3 + 2] = jnp.where(low, c0, flip(c1))
+    v2[48 + pos[1] * 3 + 2] = jnp.where(low, flip(c0), c1)
     arrive(gather_stage(0))
     arrive(gather_stage(1))
 
@@ -307,30 +322,34 @@
         s = lax.dot_general(w, high, NN, preferred_element_type=F32)
         s = s + lax.dot_general(w, less, NN, preferred_element_type=F32)
         acc = s if acc is None else acc + s
-    targets[...] = acc.reshape(12, 8, BLK)
+    targets[...] = acc.reshape(10, 8, BLK)
+    sib_w1 = send(targets.at[8 + other], sib_cross.at[1], sib_send.at[2], sib_recv.at[2], sibling)
 
     form = jnp.zeros((8, BLK), F32)
     for i in range(4):
         wa = targets[2 * i]
-        ya = apply(split(targets[2 * i + 1]), 4 + i, NT)
+        ya = apply(split(targets[2 * i + 1]), 2 + i, NT)
         dense[i, 0] = ya
         form = form + 2.0 * (wa * ya)
+    form = jnp.where((row >> 2) == core, form, 0.0)
+    sib_w1.wait_recv()
+    mine, theirs = targets[8 + core], sib_cross[1]
+    c0 = jnp.where(core == 0, mine, theirs)
+    c1 = jnp.where(core == 0, theirs, mine)
+    w1s = [jnp.where(low, c0, flip(c1)), jnp.where(low, flip(c0), c1)]
+    stacks = [stack(w) for w in w1s]
     dot00, dot01, dot11 = jnp.zeros((8, BLK), F32), jnp.zeros((8, BLK), F32), jnp.zeros((8, BLK), F32)
-    for k in range(4):
-        w1 = targets[8 + k]
-        r0 = field_of(chip, k // 2, k % 2)
-        z = factor[k] * apply(split(w1), k, NN) + noise_of(k) * w1
-        packed[k] = jnp.where(low, w1, z)
+    for b in (0, 1):
+        r0, w1 = probes[b], w1s[b]
+        z = factor[b] * (4.0 * unstack(stacks[b], kh[b], kl[b], NN)) + noise[b : b + 1, :] * w1
+        diag[b] = z
         form = form + w1 * z
         dot00 = dot00 + r0 * r0
         dot01 = dot01 + r0 * w1
         dot11 = dot11 + w1 * w1
-    g2 = loads(lambda k: targets[8 + k])
-    stat_a = jnp.sum(jnp.where(low, dot01, dot11), axis=1, keepdims=True)
-    stat_b = jnp.sum(jnp.where(low, form, dot00), axis=1, keepdims=True)
-    stats = jnp.where((lane < 16) & ((row128 >> 2) == core), g2, 0.0)
-    stats = jnp.where(lane == 16 + 2 * core, stat_a, stats)
-    stats = jnp.where(lane == 17 + 2 * core, stat_b, stats)
+    stats = loads(*stacks)
+    for i, v in enumerate((dot01, dot11, form, dot00)):
+        stats = jnp.where(lane == 16 + i, jnp.sum(v, axis=1, keepdims=True), stats)
     az2[core, region] = stats
     z2 = [send(az2.at[core, region], az2.at[core, region], z2_send.at[7, 0], z2_recv.at[7, 0], sibling)]
     for d in range(1, 8):
@@ -341,11 +360,10 @@
                     z_peer(d, cc),
                 )
             )
-    sib_pack = send(packed.at[pl.ds(2 * other, 2)], sib_packed, sib_send.at[2], sib_recv.at[2], sibling)
 
     results = []
     for i in range(4):
-        yb = apply(split(targets[2 * i]), 4 + i, NN)
+        yb = apply(split(targets[2 * i]), 2 + i, NN)
         results.append(jnp.where(low, dense[i, 0], yb))
     results = jnp.concatenate(results, axis=0)
     high = results.astype(BF16)
@@ -381,7 +399,6 @@
     for n, (dy, dx) in enumerate(PLANE):
         a2.append(send(ap2.at[chip], ap2.at[chip], p2_send.at[n], p2_recv.at[n], plane_peer(dy, dx, core)))
 
-    sib_pack.wait_recv()
     waiting(landed.at[other * 16 + chip], rs_send.at[15, 0], rs_recv.at[15, 0]).wait_recv()
     for n, (dy, dx) in enumerate(PLANE):
         for cc in (0, 1):
@@ -394,27 +411,18 @@
         for i in range(1, 16):
             s = s + landed[cc * 16 + i]
         total.append(s)
-    w1s, w2s = [], []
-    for b in (0, 1):
-        mine, theirs = packed[2 * core + b], sib_packed[b]
-        c0 = jnp.where(core == 0, mine, theirs)
-        c1 = jnp.where(core == 0, theirs, mine)
-        w1s.append(jnp.where(low, c0, flip(c1)))
-        z = jnp.where(low, flip(c0), c1)
-        pair = jnp.where(low, total[0], flip(total[1])) if b == 0 else jnp.where(low, flip(total[0]), total[1])
-        w2s.append(z + pair)
+    w2s = [
+        diag[0] + jnp.where(low, total[0], flip(total[1])),
+        diag[1] + jnp.where(low, flip(total[0]), total[1]),
+    ]
 
     arrive(a2)
     t = ap2[0]
     for i in range(1, 16):
         t = t + ap2[i]
-    a0, b0 = jnp.broadcast_to(t[:, 16:17], (8, 128)), jnp.broadcast_to(t[:, 17:18], (8, 128))
-    a1, b1 = jnp.broadcast_to(t[:, 18:19], (8, 128)), jnp.broadcast_to(t[:, 19:20], (8, 128))
     squares = jnp.sum(jnp.where(lane < 16, t * t, 0.0), axis=1, keepdims=True)
-    m1 = jnp.where(low128, a0, flip(a1))
-    m2 = jnp.where(low128, flip(a0), a1)
-    m3 = jnp.where(low128, b0, flip(b1)) + squares
-    m0 = jnp.where(low128, flip(b0), b1)
+    m1, m2, m3, m0 = [jnp.broadcast_to(t[:, 16 + i : 17 + i], (8, 128)) for i in range(4)]
+    m3 = m3 + squares
     alpha = m0 / m1
     fresh = m0 - 2.0 * alpha * m1 + alpha * alpha * m2
     grow = 1.0 + fresh / m0
@@ -424,62 +432,69 @@
     cb = (alpha * alpha2)[:, 0:1]
     for b in (0, 1):
         r0, w1 = probes[b], w1s[b]
-        f = features[b]
-        w2 = w2s[b]
-        for i in range(16):
-            w2 = w2 + t[:, i : i + 1] * f[i : i + 1, :]
-        out_sol[b] = ca * r0 - cb * w1
-        out_res[b] = r0 - ca * w1 + cb * w2
+        w2 = spread(t, features[b], w2s[b])
+        out[0, b] = ca * r0 - cb * w1
+        out[1, b] = r0 - ca * w1 + cb * w2
     for c in sends:
         c.wait_send()
 
 
 def shards(probes, coords, features, noise_var, inv_scale, owner_map, block_pairs):
     vmem = pl.BlockSpec(memory_space=pltpu.VMEM)
-    smem = pl.BlockSpec(memory_space=pltpu.SMEM)
     dma = pltpu.SemaphoreType.DMA
-    out = jax.ShapeDtypeStruct(probes.shape, F32)
+    out = jax.ShapeDtypeStruct((2,) + probes.shape, F32)
     coords = jnp.transpose(coords, (1, 0, 2))
     block_pairs = jnp.transpose(block_pairs, (0, 2, 1))
     pairs_of = []
-    for shape in ((15,), (16,), (15,), (3,), (2, 2, 3), (16, 2), (7,), (15,), (8, 2), (15,)):
+    for shape in ((15,), (16,), (15,), (4,), (2, 2, 3), (16, 2), (7,), (15,), (8, 2), (15,)):
         pairs_of += [dma(shape), dma(shape)]
-    return pl.pallas_call(
+    both = pl.pallas_call(
         kernel,
-        out_shape=(out, out),
-        in_specs=[vmem, vmem, vmem, vmem, smem, smem, smem, vmem, vmem],
-        out_specs=(vmem, vmem),
+        out_shape=out,
+        in_specs=[pl.BlockSpec(memory_space=pl.ANY)] * 7,
+        out_specs=vmem,
         scratch_shapes=[
+            pltpu.VMEM((2, 8, BLK), F32),
+            pltpu.VMEM((3, 2, BLK), F32),
+            pltpu.VMEM((2, 16, BLK), F32),
+            pltpu.VMEM((2, BLK), F32),
+            pltpu.SMEM((3,), F32),
+            pltpu.SMEM((1, 64), jnp.int32),
+            pltpu.SMEM((1, 2, 64), jnp.int32),
+            pltpu.VMEM((1, 64), jnp.int32),
+            pltpu.VMEM((1, 2, 64), jnp.int32),
+            dma((9,)),
             pltpu.VMEM((32, 8, BLK), F32),
             pltpu.VMEM((16, 2, 8, BLK), F32),
             pltpu.VMEM((2, 8, BLK), F32),
-            pltpu.VMEM((2, 16, BLK), F32),
+            pltpu.VMEM((2, 8, BLK), F32),
+            pltpu.VMEM((2, 8, BLK), F32),
             pltpu.VMEM((96, 8, BLK), F32),
             pltpu.VMEM((16, 2, 8, BLK), F32),
             pltpu.VMEM((32, 8, BLK), F32),
-            pltpu.VMEM((8, BLK, BLK), BF16),
-            pltpu.VMEM((8, BLK, BLK), BF16),
+            pltpu.VMEM((6, BLK, BLK), BF16),
+            pltpu.VMEM((6, BLK, BLK), BF16),
             pltpu.VMEM((BLK, 8), F32),
-            pltpu.VMEM((4, 16, BLK), BF16),
-            pltpu.VMEM((4, 16, BLK), BF16),
-            pltpu.VMEM((96, 768), F32),
-            pltpu.VMEM((96, 768), BF16),
-            pltpu.VMEM((4, 8, BLK), F32),
-            pltpu.VMEM((12, 8, BLK), F32),
-            pltpu.VMEM((4, 8, BLK), F32),
+            pltpu.VMEM((2, 16, BLK), BF16),
+            pltpu.VMEM((2, 16, BLK), BF16),
+            pltpu.VMEM((80, 768), F32),
+            pltpu.VMEM((80, 768), BF16),
             pltpu.VMEM((2, 8, BLK), F32),
+            pltpu.VMEM((10, 8, BLK), F32),
             pltpu.VMEM((8, 128), F32),
             pltpu.VMEM((8, 8, 128), F32),
+            pltpu.VMEM((2, 8, 128), F32),
             pltpu.VMEM((16, 8, 128), F32),
             pltpu.VMEM((2, 8, 8, 128), F32),
             pltpu.VMEM((16, 8, 128), F32),
         ]
         + pairs_of,
         compiler_params=pltpu.CompilerParams(
-            collective_id=0, has_side_effects=True, vmem_limit_bytes=40 << 20
+            collective_id=0, has_side_effects=True, vmem_limit_bytes=62 << 20
         ),
         name="cg2",
-    )(probes, coords, features, noise_var, inv_scale, owner_map, block_pairs, owner_map, block_pairs)
+    )(probes, coords, features, noise_var, inv_scale, owner_map, block_pairs)
+    return both[0], both[1]
 
 
 def solution(mesh):

time: 67.5 us -> 58.6 us (0.87)
  Pallas kernels: 61.7 us -> 56.3 us
  local copies, waits for them, and re-layouts: 4.89 us -> 1.41 us
    pallas_call x1, Pallas kernels: 61.7 us -> 56.3 us  [shards(): pl.pallas_call(kernel, out_shape=out, in_specs=[pl.BlockSpec(memory_space...]
    unnamed x16 -> x0, local copies, waits for them, and re-layouts: 4.89 us -> none
    squeeze x0 -> x1, local copies, waits for them, and re-layouts: none -> 1.41 us  [shards(): return (both[0], both[1])]
where the time goes in v3:
time: 58.6 us; the launch traced here: 58.4 us
  Pallas kernels  56.3 us (96%)
  local copies, waits for them, and re-layouts  1.41 us (2%)
  between operations  0.64 us (1%)
    pallas_call x1, Pallas kernels, shards(): pl.pallas_call(kernel, out_shape=out, in_specs=[pl.BlockSpec(memory_space...  56.3 us
    squeeze x1, local copies, waits for them, and re-layouts, shards(): return (both[0], both[1])  1.41 us

profile of v3, /device:TPU:1, one launch (start us, length us, event | category | flops | bytes accessed | tf_op | source)
XLA Modules:
  0.0 58.4 jit_solution(5980258067707687131)
XLA Ops:
  0.6 56.3 %cg2.1 = f32[2,2,8,512]{3,2,1,0:T(8,128)} custom-call(f32[2,8,512]{2,1,0:T(8,128)} %probes_in.1, f32[3,2,512]{2,1,0:T(2,128)} %bitcast.6, f32[2,16,512]{2,1,0:T(8,128)} %features_in.1, f32[2,512]{1,0:T(2,128)} %noise_in.1, f32[3]{0:T(128)} %inv_scale_in.1, s32[1,64]{1,0:T(1,128)} %owner_in.1, s32[1,2,64]{2,1,0:T(2,128)} %bitcast.7), custom_call_target="tpu_custom_call" | custom-call | tf_op jit(solution)/shard_map/cg2/pallas_call | solution.py:451
  57.0 1.4 %slice_bitcast_fusion = (f32[2,8,512]{2,1,0:T(8,128)}, f32[2,8,512]{2,1,0:T(8,128)}) fusion(f32[2,2,8,512]{3,2,1,0:T(8,128)} %cg2.1), kind=kLoop, calls=%fused_computation | loop fusion | bytes 131072 | tf_op jit(solution)/shard_map/squeeze | solution.py:497

commit v4 on v3

--- a/solution.py
+++ b/solution.py
@@ -18,9 +18,9 @@
     probes_in, coords_in, features_in, noise_in, inv_scale_in, owner_in, pairs_in,
     out,
     probes, coords, features, noise, inv_scale, owner_s, pairs_s, owner_v, pairs_v, in_sem,
-    points, field, halves, cross, sib_cross, v2, dense, landed, kh, kl, turned, fh, fl, w2f, w2b, diag, targets,
+    points, field, halves, cross, sib_cross, vp, vd, dense, landed, kh, kl, turned, fh, fl, w2f, w2b, diag, targets,
     tile, az1, ac1, ap1, az2, ap2,
-    pt_send, pt_recv, pf_send, pf_recv, fd_send, fd_recv, sib_send, sib_recv, ag_send, ag_recv,
+    pt_send, pt_recv, pf_send, pf_recv, sib_send, sib_recv, ag_send, ag_recv,
     rs_send, rs_recv, z1_send, z1_recv, p1_send, p1_recv, z2_send, z2_recv, p2_send, p2_recv,
 ):
     region = lax.axis_index("region")
@@ -41,6 +41,13 @@
 
     sibling = (region, chip * 2 + other)
 
+    barrier = pltpu.get_barrier_semaphore()
+    for dy, dx in PLANE:
+        pl.semaphore_signal(barrier, inc=1, device_id=plane_peer(dy, dx, core), device_id_type=MESH)
+    for d in range(1, 8):
+        pl.semaphore_signal(barrier, inc=1, device_id=z_peer(d, core), device_id_type=MESH)
+    pl.semaphore_signal(barrier, inc=1, device_id=sibling, device_id_type=MESH)
+
     loads_in = []
     for src, dst in (
         (coords_in, coords), (noise_in, noise), (probes_in, probes), (features_in, features), (inv_scale_in, inv_scale),
@@ -50,13 +57,6 @@
         c.start()
         loads_in.append(c)
 
-    barrier = pltpu.get_barrier_semaphore()
-    for dy, dx in PLANE:
-        pl.semaphore_signal(barrier, inc=1, device_id=plane_peer(dy, dx, core), device_id_type=MESH)
-    for d in range(1, 8):
-        pl.semaphore_signal(barrier, inc=1, device_id=z_peer(d, core), device_id_type=MESH)
-    pl.semaphore_signal(barrier, inc=1, device_id=sibling, device_id_type=MESH)
-
     row = lax.broadcasted_iota(jnp.int32, (8, BLK), 0)
     low = row < 4
     lane = lax.broadcasted_iota(jnp.int32, (8, 128), 1)
@@ -66,7 +66,7 @@
     def flip(v):
         return pltpu.roll(v, 4, 0)
 
-    for c in loads_in:
+    for c in loads_in[:3]:
         c.wait()
     here = core * 16 + chip
     for b in (0, 1):
@@ -76,7 +76,7 @@
     p0, p1 = probes[0], probes[1]
     halves[0] = jnp.where(low, p0, flip(p1))
     halves[1] = jnp.where(low, flip(p0), p1)
-    field[chip, core] = halves[core]
+    field[core * 16 + lax.select(core == 0, pos[0], pos[1])] = halves[core]
 
     pl.semaphore_wait(barrier, 23)
 
@@ -90,11 +90,17 @@
         sends.append(c)
         return c
 
+    def drain():
+        for c in sends:
+            c.wait_send()
+        sends.clear()
+
     def arrive(copies):
         for c in copies:
             c.wait_recv()
 
-    sib_field = send(halves.at[other], field.at[chip, core], sib_send.at[0], sib_recv.at[0], sibling)
+    own_field = field.at[core * 16 + lax.select(core == 0, pos[0], pos[1])]
+    sib_field = send(halves.at[other], own_field, sib_send.at[0], sib_recv.at[0], sibling)
     point_copies = []
     for n, (dy, dx) in enumerate(PLANE):
         point_copies.append(
@@ -102,6 +108,25 @@
         )
     forwards = [send(points.at[here], points.at[here], pf_send.at[15], pf_recv.at[15], sibling)]
 
+    def gather_stage(buf, m, call, stage_index):
+        out = []
+        for h in (0, 1):
+            if stage_index == 0:
+                span = pl.ds(h * 16 * m + pos[h] * m, m)
+                steps = [(0, d) if h == 0 else (d, 0) for d in (1, 2, 3)]
+            else:
+                span = pl.ds(h * 16 * m + (y, x)[h] * 4 * m, 4 * m)
+                steps = [(d, 0) if h == 0 else (0, d) for d in (1, 2, 3)]
+            for d, (dy, dx) in enumerate(steps):
+                sem = (call, stage_index, h, d)
+                out.append(send(buf.at[span], buf.at[span], ag_send.at[sem], ag_recv.at[sem], plane_peer(dy, dx, core)))
+        return out
+
+    sib_field.wait_recv()
+    field_first = gather_stage(field, 1, 0, 0)
+
+    for c in loads_in[3:]:
+        c.wait()
     sx, sy, st = inv_scale[0], inv_scale[1], inv_scale[2]
 
     def make_tile(index, left, right):
@@ -135,7 +160,7 @@
         return jnp.where(b == 0, v, flip(v))
 
     def field_of(q, c, b):
-        v = field[q, c]
+        v = field[c * 16 + jnp.where(c == 0, q, (q & 3) * 4 + (q >> 2))]
         f = flip(v)
         first, second = jnp.where(low, v, f), jnp.where(low, f, v)
         if isinstance(b, int):
@@ -180,17 +205,13 @@
     for d in range(1, 8):
         z1.append(send(az1.at[region], az1.at[region], z1_send.at[d - 1], z1_recv.at[d - 1], z_peer(d, core)))
 
-    sib_field.wait_recv()
-    field_copies = []
-    for n, (dy, dx) in enumerate(PLANE):
-        field_copies.append(
-            send(field.at[chip], field.at[chip], fd_send.at[n], fd_recv.at[n], plane_peer(dy, dx, core))
-        )
-
     mine0 = points[here]
     make_tile(0, mine0, mine0)
     mine1 = flip(mine0)
     make_tile(1, mine1, mine1)
+
+    arrive(field_first)
+    field_second = gather_stage(field, 1, 0, 1)
 
     lane64 = lax.broadcasted_iota(jnp.int32, (64, 64), 1)
     owner_row = owner_v[...].astype(F32)
@@ -205,14 +226,14 @@
     j = lax.broadcasted_iota(jnp.int32, (1, 768), 1)
     n = j >> 3
     side = (j >> 2) & 1
-    h = (n >= 48).astype(jnp.int32)
-    rest = n - h * 48
-    place = (rest * 171) >> 9
-    e = rest - place * 3
+    is_pair = n < 64
+    h = jnp.where(is_pair, n >> 5, (n >> 4) & 1)
+    place = jnp.where(is_pair, (n & 31) >> 1, n & 15)
+    e = n & 1
     q = jnp.where(h == 0, place, (place & 3) * 4 + (place >> 2))
     pick = lax.broadcasted_iota(jnp.int32, (64, 768), 0) == q * 4 + h * 2 + e
     listed = jnp.sum(jnp.where(pick, jnp.where(side == 0, slot_a, slot_b), 0.0), axis=0, keepdims=True)
-    lanes2 = jnp.where(e == 2, (q * 4 + side * 2 + h).astype(F32), listed)
+    lanes2 = jnp.where(is_pair, listed, (q * 4 + side * 2 + h).astype(F32))
     same_column = (lax.broadcasted_iota(jnp.int32, (8, 768), 0) & 3) == (j & 3)
     wanted = []
     for i in range(4):
@@ -267,6 +288,15 @@
         qb, cb, bb = where_is(second[i])
         make_tile(2 + i, points_of(ca * 16 + qa, ba), points_of(cb * 16 + qb, bb))
 
+    arrive(field_second)
+    for i in range(4):
+        va, vb = field_of(*where_is(first[i])), field_of(*where_is(second[i]))
+        ya = apply(split(vb), 2 + i, NT)
+        yb = apply(split(va), 2 + i, NN)
+        vp[(i // 2) * 32 + pos[i // 2] * 2 + i % 2] = jnp.where(low, ya, yb)
+
+    pair_first = gather_stage(vp, 2, 1, 0)
+
     arrive(a1)
     g1 = ap1[0]
     for i in range(1, 16):
@@ -282,40 +312,28 @@
     cross[0] = jnp.where(low, d0, flip(d1))
     cross[1] = jnp.where(low, flip(d0), d1)
     sib_diag = send(cross.at[other], sib_cross.at[0], sib_send.at[1], sib_recv.at[1], sibling)
-
-    arrive(field_copies)
-    for i in range(4):
-        va, vb = field_of(*where_is(first[i])), field_of(*where_is(second[i]))
-        ya = apply(split(vb), 2 + i, NT)
-        yb = apply(split(va), 2 + i, NN)
-        v2[(i // 2) * 48 + pos[i // 2] * 3 + i % 2] = jnp.where(low, ya, yb)
-
-    def gather_stage(stage_index):
-        out = []
-        for h in (0, 1):
-            if stage_index == 0:
-                span = pl.ds(h * 48 + pos[h] * 3, 3)
-                steps = [(0, d) if h == 0 else (d, 0) for d in (1, 2, 3)]
-            else:
-                span = pl.ds(h * 48 + (y, x)[h] * 12, 12)
-                steps = [(d, 0) if h == 0 else (0, d) for d in (1, 2, 3)]
-            for d, (dy, dx) in enumerate(steps):
-                sem = (stage_index, h, d)
-                out.append(send(v2.at[span], v2.at[span], ag_send.at[sem], ag_recv.at[sem], plane_peer(dy, dx, core)))
-        return out
-
     sib_diag.wait_recv()
     mine, theirs = cross[core], sib_cross[0]
     c0 = jnp.where(core == 0, mine, theirs)
     c1 = jnp.where(core == 0, theirs, mine)
-    v2[pos[0] * 3 + 2] = jnp.where(low, c0, flip(c1))
-    v2[48 + pos[1] * 3 + 2] = jnp.where(low, flip(c0), c1)
-    arrive(gather_stage(0))
-    arrive(gather_stage(1))
+    vd[pos[0]] = jnp.where(low, c0, flip(c1))
+    vd[16 + pos[1]] = jnp.where(low, flip(c0), c1)
+    diag_first = gather_stage(vd, 1, 2, 0)
+    arrive(pair_first)
+    older = list(sends)
+    sends.clear()
+    pair_second = gather_stage(vp, 2, 1, 1)
+    arrive(diag_first)
+    diag_second = gather_stage(vd, 1, 2, 1)
+    for c in older:
+        c.wait_send()
+    arrive(pair_second)
+    arrive(diag_second)
 
     acc = None
     for lo_row in range(0, 768, 256):
-        part = v2[lo_row // 8 : lo_row // 8 + 32].reshape(256, BLK)
+        part = vp[lo_row // 8 : lo_row // 8 + 32] if lo_row < 512 else vd[...]
+        part = part.reshape(256, BLK)
         w = w2b[:, lo_row : lo_row + 256]
         high = part.astype(BF16)
         less = (part - high.astype(F32)).astype(BF16)
@@ -350,16 +368,12 @@
     stats = loads(*stacks)
     for i, v in enumerate((dot01, dot11, form, dot00)):
         stats = jnp.where(lane == 16 + i, jnp.sum(v, axis=1, keepdims=True), stats)
-    az2[core, region] = stats
-    z2 = [send(az2.at[core, region], az2.at[core, region], z2_send.at[7, 0], z2_recv.at[7, 0], sibling)]
-    for d in range(1, 8):
-        for cc in (0, 1):
-            z2.append(
-                send(
-                    az2.at[core, region], az2.at[core, region], z2_send.at[d - 1, cc], z2_recv.at[d - 1, core],
-                    z_peer(d, cc),
-                )
-            )
+    ap2[chip] = stats
+    older2 = list(sends)
+    sends.clear()
+    a2 = []
+    for n, (dy, dx) in enumerate(PLANE):
+        a2.append(send(ap2.at[chip], ap2.at[chip], p2_send.at[n], p2_recv.at[n], plane_peer(dy, dx, core)))
 
     results = []
     for i in range(4):
@@ -385,19 +399,24 @@
             src_ref=dst, dst_ref=dst, send_sem=ssem, recv_sem=rsem, device_id=sibling, device_id_type=MESH
         )
 
-    z2[0].wait_recv()
+    for c in older2:
+        c.wait_send()
+    arrive(a2)
+    t = ap2[0]
+    for i in range(1, 16):
+        t = t + ap2[i]
+    az2[core, region] = t
+    older3 = list(sends)
+    sends.clear()
+    z2 = [send(az2.at[core, region], az2.at[core, region], z2_send.at[7, 0], z2_recv.at[7, 0], sibling)]
     for d in range(1, 8):
         for cc in (0, 1):
-            waiting(
-                az2.at[cc, lax.rem(region + 8 - d, 8)], z2_send.at[d - 1, cc], z2_recv.at[d - 1, cc]
-            ).wait_recv()
-    t = az2[0, 0]
-    for i in range(1, 16):
-        t = t + az2[i // 8, i % 8]
-    ap2[chip] = t
-    a2 = []
-    for n, (dy, dx) in enumerate(PLANE):
-        a2.append(send(ap2.at[chip], ap2.at[chip], p2_send.at[n], p2_recv.at[n], plane_peer(dy, dx, core)))
+            z2.append(
+                send(
+                    az2.at[core, region], az2.at[core, region], z2_send.at[d - 1, cc], z2_recv.at[d - 1, core],
+                    z_peer(d, cc),
+                )
+            )
 
     waiting(landed.at[other * 16 + chip], rs_send.at[15, 0], rs_recv.at[15, 0]).wait_recv()
     for n, (dy, dx) in enumerate(PLANE):
@@ -416,10 +435,17 @@
         diag[1] + jnp.where(low, flip(total[0]), total[1]),
     ]
 
-    arrive(a2)
-    t = ap2[0]
+    for c in older3:
+        c.wait_send()
+    z2[0].wait_recv()
+    for d in range(1, 8):
+        for cc in (0, 1):
+            waiting(
+                az2.at[cc, lax.rem(region + 8 - d, 8)], z2_send.at[d - 1, cc], z2_recv.at[d - 1, cc]
+            ).wait_recv()
+    t = az2[0, 0]
     for i in range(1, 16):
-        t = t + ap2[i]
+        t = t + az2[i // 8, i % 8]
     squares = jnp.sum(jnp.where(lane < 16, t * t, 0.0), axis=1, keepdims=True)
     m1, m2, m3, m0 = [jnp.broadcast_to(t[:, 16 + i : 17 + i], (8, 128)) for i in range(4)]
     m3 = m3 + squares
@@ -435,18 +461,17 @@
         w2 = spread(t, features[b], w2s[b])
         out[0, b] = ca * r0 - cb * w1
         out[1, b] = r0 - ca * w1 + cb * w2
-    for c in sends:
-        c.wait_send()
+    drain()
 
 
 def shards(probes, coords, features, noise_var, inv_scale, owner_map, block_pairs):
     vmem = pl.BlockSpec(memory_space=pltpu.VMEM)
     dma = pltpu.SemaphoreType.DMA
-    out = jax.ShapeDtypeStruct((2,) + probes.shape, F32)
+    out = pltpu.VMEM((2,) + probes.shape, F32)
     coords = jnp.transpose(coords, (1, 0, 2))
     block_pairs = jnp.transpose(block_pairs, (0, 2, 1))
     pairs_of = []
-    for shape in ((15,), (16,), (15,), (4,), (2, 2, 3), (16, 2), (7,), (15,), (8, 2), (15,)):
+    for shape in ((15,), (16,), (4,), (3, 2, 2, 3), (16, 2), (7,), (15,), (8, 2), (15,)):
         pairs_of += [dma(shape), dma(shape)]
     both = pl.pallas_call(
         kernel,
@@ -465,11 +490,12 @@
             pltpu.VMEM((1, 2, 64), jnp.int32),
             dma((9,)),
             pltpu.VMEM((32, 8, BLK), F32),
-            pltpu.VMEM((16, 2, 8, BLK), F32),
+            pltpu.VMEM((32, 8, BLK), F32),
             pltpu.VMEM((2, 8, BLK), F32),
             pltpu.VMEM((2, 8, BLK), F32),
             pltpu.VMEM((2, 8, BLK), F32),
-            pltpu.VMEM((96, 8, BLK), F32),
+            pltpu.VMEM((64, 8, BLK), F32),
+            pltpu.VMEM((32, 8, BLK), F32),
             pltpu.VMEM((16, 2, 8, BLK), F32),
             pltpu.VMEM((32, 8, BLK), F32),
             pltpu.VMEM((6, BLK, BLK), BF16),

time: 58.6 us -> 55.6 us (0.949)
  Pallas kernels: 56.3 us -> 54.2 us
  local copies, waits for them, and re-layouts: 1.41 us -> 0.63 us
    pallas_call x1, Pallas kernels: 56.3 us -> 54.2 us  [shards(): pl.pallas_call(kernel, out_shape=out, in_specs=[pl.BlockSpec(memory_space...]
    squeeze x1, local copies, waits for them, and re-layouts: 1.41 us -> 0.63 us  [shards(): return (both[0], both[1])]
where the time goes in v4:
time: 55.6 us; the launch traced here: 55.5 us
  Pallas kernels  54.2 us (97%)
  between operations  0.64 us (1%)
  local copies, waits for them, and re-layouts  0.63 us (1%)
    pallas_call x1, Pallas kernels, shards(): pl.pallas_call(kernel, out_shape=out, in_specs=[pl.BlockSpec(memory_space...  54.2 us

profile of v4, /device:TPU:1, one launch (start us, length us, event | category | flops | bytes accessed | tf_op | source)
XLA Modules:
  0.0 55.5 jit_solution(6533965812920874261)
XLA Ops:
  0.6 54.2 %cg2.1 = f32[2,2,8,512]{3,2,1,0:T(8,128)S(1)} custom-call(f32[2,8,512]{2,1,0:T(8,128)} %probes_in.1, f32[3,2,512]{2,1,0:T(2,128)} %bitcast.6, f32[2,16,512]{2,1,0:T(8,128)} %features_in.1, f32[2,512]{1,0:T(2,128)} %noise_in.1, f32[3]{0:T(128)} %inv_scale_in.1, s32[1,64]{1,0:T(1,128)} %owner_in.1, s32[1,2,64]{2,1,0:T(2,128)} %bitcast.7), custom_call_target="tpu_custom_call" | custom-call | tf_op jit(solution)/shard_map/cg2/pallas_call | solution.py:476
  54.8 0.6 %slice_bitcast_fusion = (f32[2,8,512]{2,1,0:T(8,128)}, f32[2,8,512]{2,1,0:T(8,128)}) fusion(f32[2,2,8,512]{3,2,1,0:T(8,128)S(1)} %cg2.1), kind=kLoop, calls=%fused_computation | loop fusion | bytes 131072 | tf_op jit(solution)/shard_map/squeeze | solution.py:523

commit v5 on v4

--- a/solution.py
+++ b/solution.py
@@ -13,6 +13,26 @@
 NN = (((1,), (0,)), ((), ()))
 PLANE = [(dy, dx) for dy in range(4) for dx in range(4) if dy or dx]
 
+GROUPS = (
+    "sib_field",
+    "points",
+    "field_first",
+    "z1",
+    "field_second",
+    "sib_loads",
+    "forward",
+    "a1",
+    "pair_first",
+    "sib_diag",
+    "diag_first",
+    "pair_second",
+    "diag_second",
+    "sib_w1",
+    "a2",
+    "results",
+    "z2",
+)
+
 
 def kernel(
     probes_in, coords_in, features_in, noise_in, inv_scale_in, owner_in, pairs_in,
@@ -20,8 +40,7 @@
     probes, coords, features, noise, inv_scale, owner_s, pairs_s, owner_v, pairs_v, in_sem,
     points, field, halves, cross, sib_cross, vp, vd, dense, landed, kh, kl, turned, fh, fl, w2f, w2b, diag, targets,
     tile, az1, ac1, ap1, az2, ap2,
-    pt_send, pt_recv, pf_send, pf_recv, sib_send, sib_recv, ag_send, ag_recv,
-    rs_send, rs_recv, z1_send, z1_recv, p1_send, p1_recv, z2_send, z2_recv, p2_send, p2_recv,
+    group_send, group_recv,
 ):
     region = lax.axis_index("region")
     dev = lax.axis_index("dev")
@@ -80,36 +99,35 @@
 
     pl.semaphore_wait(barrier, 23)
 
-    sends = []
-
-    def send(src, dst, ssem, rsem, device):
-        c = pltpu.make_async_remote_copy(
-            src_ref=src, dst_ref=dst, send_sem=ssem, recv_sem=rsem, device_id=device, device_id_type=MESH
+    def send(group, src, dst, device):
+        pltpu.make_async_remote_copy(
+            src_ref=src, dst_ref=dst, send_sem=group_send.at[GROUPS.index(group)], recv_sem=group_recv.at[GROUPS.index(group)],
+            device_id=device, device_id_type=MESH,
+        ).start()
+
+    def whole(group, span):
+        return pltpu.make_async_remote_copy(
+            src_ref=span, dst_ref=span, send_sem=group_send.at[GROUPS.index(group)], recv_sem=group_recv.at[GROUPS.index(group)],
+            device_id=sibling, device_id_type=MESH,
         )
-        c.start()
-        sends.append(c)
-        return c
-
-    def drain():
-        for c in sends:
-            c.wait_send()
-        sends.clear()
-
-    def arrive(copies):
-        for c in copies:
-            c.wait_recv()
+
+    spans = {}
+
+    def arrive(group):
+        whole(group, spans[group]).wait_recv()
+
+    def sent(*groups):
+        for group in groups:
+            whole(group, spans[group]).wait_send()
 
     own_field = field.at[core * 16 + lax.select(core == 0, pos[0], pos[1])]
-    sib_field = send(halves.at[other], own_field, sib_send.at[0], sib_recv.at[0], sibling)
-    point_copies = []
-    for n, (dy, dx) in enumerate(PLANE):
-        point_copies.append(
-            send(points.at[here], points.at[here], pt_send.at[n], pt_recv.at[n], plane_peer(dy, dx, core))
-        )
-    forwards = [send(points.at[here], points.at[here], pf_send.at[15], pf_recv.at[15], sibling)]
-
-    def gather_stage(buf, m, call, stage_index):
-        out = []
+    send("sib_field", halves.at[other], own_field, sibling)
+    spans["sib_field"] = halves.at[0]
+    for dy, dx in PLANE:
+        send("points", points.at[here], points.at[here], plane_peer(dy, dx, core))
+    spans["points"] = points.at[pl.ds(0, 15)]
+
+    def gather_stage(name, buf, m, stage_index):
         for h in (0, 1):
             if stage_index == 0:
                 span = pl.ds(h * 16 * m + pos[h] * m, m)
@@ -117,13 +135,12 @@
             else:
                 span = pl.ds(h * 16 * m + (y, x)[h] * 4 * m, 4 * m)
                 steps = [(d, 0) if h == 0 else (0, d) for d in (1, 2, 3)]
-            for d, (dy, dx) in enumerate(steps):
-                sem = (call, stage_index, h, d)
-                out.append(send(buf.at[span], buf.at[span], ag_send.at[sem], ag_recv.at[sem], plane_peer(dy, dx, core)))
-        return out
-
-    sib_field.wait_recv()
-    field_first = gather_stage(field, 1, 0, 0)
+            for dy, dx in steps:
+                send(name, buf.at[span], buf.at[span], plane_peer(dy, dx, core))
+        spans[name] = buf.at[pl.ds(0, 6 * m * (1 if stage_index == 0 else 4))]
+
+    arrive("sib_field")
+    gather_stage("field_first", field, 1, 0)
 
     for c in loads_in[3:]:
         c.wait()
@@ -201,17 +218,17 @@
     tile[...] = jnp.zeros_like(tile)
     first_stack = [stack(probes[b]) for b in (0, 1)]
     az1[region] = loads(*first_stack)
-    z1 = []
     for d in range(1, 8):
-        z1.append(send(az1.at[region], az1.at[region], z1_send.at[d - 1], z1_recv.at[d - 1], z_peer(d, core)))
+        send("z1", az1.at[region], az1.at[region], z_peer(d, core))
+    spans["z1"] = az1.at[pl.ds(0, 7)]
 
     mine0 = points[here]
     make_tile(0, mine0, mine0)
     mine1 = flip(mine0)
     make_tile(1, mine1, mine1)
 
-    arrive(field_first)
-    field_second = gather_stage(field, 1, 0, 1)
+    arrive("field_first")
+    gather_stage("field_second", field, 1, 1)
 
     lane64 = lax.broadcasted_iota(jnp.int32, (64, 64), 1)
     owner_row = owner_v[...].astype(F32)
@@ -223,6 +240,81 @@
         first.append(owner_s[0, pairs_s[0, 0, chip * 4 + i]])
         second.append(owner_s[0, pairs_s[0, 1, chip * 4 + i]])
 
+    wanted = []
+    for i in range(4):
+        wanted += [first[i], second[i]]
+    factor = []
+    for b in (0, 1):
+        me = (dev * 2 + b).astype(F32)
+        count = jnp.where(slot_a == me, 1.0, 0.0) + jnp.where(slot_b == me, 1.0, 0.0)
+        factor.append(1.0 + jnp.sum(count, axis=0, keepdims=True))
+    arrive("z1")
+    t = az1[0]
+    for i in range(1, 8):
+        t = t + az1[i]
+    ac1[0] = t
+    send("sib_loads", ac1.at[0], ac1.at[1], sibling)
+    spans["sib_loads"] = ac1.at[0]
+    arrive("points")
+    slab = points.at[pl.ds(core * 16, 16)]
+    send("forward", slab, slab, sibling)
+    spans["forward"] = slab
+
+    arrive("sib_loads")
+    ap1[chip] = ac1[0] + ac1[1]
+    for dy, dx in PLANE:
+        send("a1", ap1.at[chip], ap1.at[chip], plane_peer(dy, dx, core))
+    spans["a1"] = ap1.at[pl.ds(0, 15)]
+
+    for b in (0, 1):
+        diag[b] = factor[b] * (4.0 * unstack(first_stack[b], kh[b], kl[b], NN)) + noise[b : b + 1, :] * probes[b]
+
+    arrive("forward")
+
+    def where_is(s):
+        return s >> 2, (s >> 1) & 1, s & 1
+
+    for i in range(4):
+        qa, ca, ba = where_is(first[i])
+        qb, cb, bb = where_is(second[i])
+        make_tile(2 + i, points_of(ca * 16 + qa, ba), points_of(cb * 16 + qb, bb))
+
+    arrive("field_second")
+    for i in range(4):
+        va, vb = field_of(*where_is(first[i])), field_of(*where_is(second[i]))
+        ya = apply(split(vb), 2 + i, NT)
+        yb = apply(split(va), 2 + i, NN)
+        vp[(i // 2) * 32 + pos[i // 2] * 2 + i % 2] = jnp.where(low, ya, yb)
+
+    gather_stage("pair_first", vp, 2, 0)
+
+    arrive("a1")
+    g1 = ap1[0]
+    for i in range(1, 16):
+        g1 = g1 + ap1[i]
+
+    def spread(g, f, acc):
+        for i in range(16):
+            acc = acc + g[:, i : i + 1] * f[i : i + 1, :]
+        return acc
+
+    d0 = spread(g1, features[0], diag[0])
+    d1 = spread(g1, features[1], diag[1])
+    cross[0] = jnp.where(low, d0, flip(d1))
+    cross[1] = jnp.where(low, flip(d0), d1)
+    send("sib_diag", cross.at[other], sib_cross.at[0], sibling)
+    spans["sib_diag"] = cross.at[0]
+    arrive("sib_diag")
+    mine, theirs = cross[core], sib_cross[0]
+    c0 = jnp.where(core == 0, mine, theirs)
+    c1 = jnp.where(core == 0, theirs, mine)
+    vd[pos[0]] = jnp.where(low, c0, flip(c1))
+    vd[16 + pos[1]] = jnp.where(low, flip(c0), c1)
+    gather_stage("diag_first", vd, 1, 0)
+    arrive("pair_first")
+    gather_stage("pair_second", vp, 2, 1)
+    arrive("diag_first")
+    gather_stage("diag_second", vd, 1, 1)
     j = lax.broadcasted_iota(jnp.int32, (1, 768), 1)
     n = j >> 3
     side = (j >> 2) & 1
@@ -235,9 +327,6 @@
     listed = jnp.sum(jnp.where(pick, jnp.where(side == 0, slot_a, slot_b), 0.0), axis=0, keepdims=True)
     lanes2 = jnp.where(is_pair, listed, (q * 4 + side * 2 + h).astype(F32))
     same_column = (lax.broadcasted_iota(jnp.int32, (8, 768), 0) & 3) == (j & 3)
-    wanted = []
-    for i in range(4):
-        wanted += [first[i], second[i]]
     for k in range(8):
         hit = (lanes2 == wanted[k].astype(F32)) & same_column
         w2f[8 * k : 8 * k + 8, :] = jnp.where(hit, 1.0, 0.0)
@@ -246,89 +335,16 @@
         hit = (lanes2 == (chip * 4 + 2 * k + block_of_row).astype(F32)) & same_column
         w2f[64 + 8 * k : 72 + 8 * k, :] = jnp.where(hit, 1.0, 0.0)
     w2b[...] = w2f[...].astype(BF16)
-    factor = []
-    for b in (0, 1):
-        me = (dev * 2 + b).astype(F32)
-        count = jnp.where(slot_a == me, 1.0, 0.0) + jnp.where(slot_b == me, 1.0, 0.0)
-        factor.append(1.0 + jnp.sum(count, axis=0, keepdims=True))
     lane32 = lax.broadcasted_iota(jnp.int32, (256, 32), 1)
     slot32 = jnp.zeros((256, 32), jnp.int32)
     for i in range(8):
         slot32 = jnp.where((lane32 >> 2) == i, wanted[i], slot32)
     row32 = lax.broadcasted_iota(jnp.int32, (256, 32), 0)
     w3 = jnp.where((slot32 == (row32 >> 2)) & ((lane32 & 3) == (row32 & 3)), 1.0, 0.0).astype(BF16)
-
-    arrive(z1)
-    t = az1[0]
-    for i in range(1, 8):
-        t = t + az1[i]
-    ac1[0] = t
-    sib_loads = send(ac1.at[0], ac1.at[1], sib_send.at[3], sib_recv.at[3], sibling)
-    for n, (dy, dx) in enumerate(PLANE):
-        back = core * 16 + plane_chip(-dy % 4, -dx % 4)
-        point_copies[n].wait_recv()
-        forwards.append(send(points.at[back], points.at[back], pf_send.at[n], pf_recv.at[n], sibling))
-
-    sib_loads.wait_recv()
-    ap1[chip] = ac1[0] + ac1[1]
-    a1 = []
-    for n, (dy, dx) in enumerate(PLANE):
-        a1.append(send(ap1.at[chip], ap1.at[chip], p1_send.at[n], p1_recv.at[n], plane_peer(dy, dx, core)))
-
-    for b in (0, 1):
-        diag[b] = factor[b] * (4.0 * unstack(first_stack[b], kh[b], kl[b], NN)) + noise[b : b + 1, :] * probes[b]
-
-    arrive(forwards)
-
-    def where_is(s):
-        return s >> 2, (s >> 1) & 1, s & 1
-
-    for i in range(4):
-        qa, ca, ba = where_is(first[i])
-        qb, cb, bb = where_is(second[i])
-        make_tile(2 + i, points_of(ca * 16 + qa, ba), points_of(cb * 16 + qb, bb))
-
-    arrive(field_second)
-    for i in range(4):
-        va, vb = field_of(*where_is(first[i])), field_of(*where_is(second[i]))
-        ya = apply(split(vb), 2 + i, NT)
-        yb = apply(split(va), 2 + i, NN)
-        vp[(i // 2) * 32 + pos[i // 2] * 2 + i % 2] = jnp.where(low, ya, yb)
-
-    pair_first = gather_stage(vp, 2, 1, 0)
-
-    arrive(a1)
-    g1 = ap1[0]
-    for i in range(1, 16):
-        g1 = g1 + ap1[i]
-
-    def spread(g, f, acc):
-        for i in range(16):
-            acc = acc + g[:, i : i + 1] * f[i : i + 1, :]
-        return acc
-
-    d0 = spread(g1, features[0], diag[0])
-    d1 = spread(g1, features[1], diag[1])
-    cross[0] = jnp.where(low, d0, flip(d1))
-    cross[1] = jnp.where(low, flip(d0), d1)
-    sib_diag = send(cross.at[other], sib_cross.at[0], sib_send.at[1], sib_recv.at[1], sibling)
-    sib_diag.wait_recv()
-    mine, theirs = cross[core], sib_cross[0]
-    c0 = jnp.where(core == 0, mine, theirs)
-    c1 = jnp.where(core == 0, theirs, mine)
-    vd[pos[0]] = jnp.where(low, c0, flip(c1))
-    vd[16 + pos[1]] = jnp.where(low, flip(c0), c1)
-    diag_first = gather_stage(vd, 1, 2, 0)
-    arrive(pair_first)
-    older = list(sends)
-    sends.clear()
-    pair_second = gather_stage(vp, 2, 1, 1)
-    arrive(diag_first)
-    diag_second = gather_stage(vd, 1, 2, 1)
-    for c in older:
-        c.wait_send()
-    arrive(pair_second)
-    arrive(diag_second)
+    sent("sib_field", "points", "field_first", "z1", "field_second", "sib_loads", "forward", "a1")
+    sent("pair_first", "sib_diag", "diag_first")
+    arrive("pair_second")
+    arrive("diag_second")
 
     acc = None
     for lo_row in range(0, 768, 256):
@@ -341,7 +357,8 @@
         s = s + lax.dot_general(w, less, NN, preferred_element_type=F32)
         acc = s if acc is None else acc + s
     targets[...] = acc.reshape(10, 8, BLK)
-    sib_w1 = send(targets.at[8 + other], sib_cross.at[1], sib_send.at[2], sib_recv.at[2], sibling)
+    send("sib_w1", targets.at[8 + other], sib_cross.at[1], sibling)
+    spans["sib_w1"] = cross.at[0]
 
     form = jnp.zeros((8, BLK), F32)
     for i in range(4):
@@ -350,7 +367,7 @@
         dense[i, 0] = ya
         form = form + 2.0 * (wa * ya)
     form = jnp.where((row >> 2) == core, form, 0.0)
-    sib_w1.wait_recv()
+    arrive("sib_w1")
     mine, theirs = targets[8 + core], sib_cross[1]
     c0 = jnp.where(core == 0, mine, theirs)
     c1 = jnp.where(core == 0, theirs, mine)
@@ -369,11 +386,9 @@
     for i, v in enumerate((dot01, dot11, form, dot00)):
         stats = jnp.where(lane == 16 + i, jnp.sum(v, axis=1, keepdims=True), stats)
     ap2[chip] = stats
-    older2 = list(sends)
-    sends.clear()
-    a2 = []
-    for n, (dy, dx) in enumerate(PLANE):
-        a2.append(send(ap2.at[chip], ap2.at[chip], p2_send.at[n], p2_recv.at[n], plane_peer(dy, dx, core)))
+    for dy, dx in PLANE:
+        send("a2", ap2.at[chip], ap2.at[chip], plane_peer(dy, dx, core))
+    spans["a2"] = ap2.at[pl.ds(0, 15)]
 
     results = []
     for i in range(4):
@@ -386,44 +401,26 @@
     s = s + lax.dot_general(w3, less, NN, preferred_element_type=F32)
     dense[...] = s.reshape(16, 2, 8, BLK)
     landed[here] = dense[chip, core]
-    send(dense.at[chip, other], landed.at[here], rs_send.at[15, 0], rs_recv.at[15, 0], sibling)
-    for n, (dy, dx) in enumerate(PLANE):
+    send("results", dense.at[chip, other], landed.at[here], sibling)
+    for dy, dx in PLANE:
         for cc in (0, 1):
-            send(
-                dense.at[plane_chip(dy, dx), cc], landed.at[here], rs_send.at[n, cc], rs_recv.at[n, core],
-                plane_peer(dy, dx, cc),
-            )
-
-    def waiting(dst, ssem, rsem):
-        return pltpu.make_async_remote_copy(
-            src_ref=dst, dst_ref=dst, send_sem=ssem, recv_sem=rsem, device_id=sibling, device_id_type=MESH
-        )
-
-    for c in older2:
-        c.wait_send()
-    arrive(a2)
+            send("results", dense.at[plane_chip(dy, dx), cc], landed.at[here], plane_peer(dy, dx, cc))
+    spans["results"] = landed.at[pl.ds(0, 31)]
+
+    sent("pair_second", "diag_second", "sib_w1")
+    arrive("a2")
     t = ap2[0]
     for i in range(1, 16):
         t = t + ap2[i]
-    az2[core, region] = t
-    older3 = list(sends)
-    sends.clear()
-    z2 = [send(az2.at[core, region], az2.at[core, region], z2_send.at[7, 0], z2_recv.at[7, 0], sibling)]
+    mine_z = core * 8 + region
+    az2[mine_z] = t
+    send("z2", az2.at[mine_z], az2.at[mine_z], sibling)
     for d in range(1, 8):
         for cc in (0, 1):
-            z2.append(
-                send(
-                    az2.at[core, region], az2.at[core, region], z2_send.at[d - 1, cc], z2_recv.at[d - 1, core],
-                    z_peer(d, cc),
-                )
-            )
-
-    waiting(landed.at[other * 16 + chip], rs_send.at[15, 0], rs_recv.at[15, 0]).wait_recv()
-    for n, (dy, dx) in enumerate(PLANE):
-        for cc in (0, 1):
-            waiting(
-                landed.at[cc * 16 + plane_chip(-dy % 4, -dx % 4)], rs_send.at[n, cc], rs_recv.at[n, cc]
-            ).wait_recv()
+            send("z2", az2.at[mine_z], az2.at[mine_z], z_peer(d, cc))
+    spans["z2"] = az2.at[pl.ds(0, 15)]
+
+    arrive("results")
     total = []
     for cc in (0, 1):
         s = landed[cc * 16]
@@ -435,17 +432,11 @@
         diag[1] + jnp.where(low, flip(total[0]), total[1]),
     ]
 
-    for c in older3:
-        c.wait_send()
-    z2[0].wait_recv()
-    for d in range(1, 8):
-        for cc in (0, 1):
-            waiting(
-                az2.at[cc, lax.rem(region + 8 - d, 8)], z2_send.at[d - 1, cc], z2_recv.at[d - 1, cc]
-            ).wait_recv()
-    t = az2[0, 0]
+    sent("a2", "results")
+    arrive("z2")
+    t = az2[0]
     for i in range(1, 16):
-        t = t + az2[i // 8, i % 8]
+        t = t + az2[i]
     squares = jnp.sum(jnp.where(lane < 16, t * t, 0.0), axis=1, keepdims=True)
     m1, m2, m3, m0 = [jnp.broadcast_to(t[:, 16 + i : 17 + i], (8, 128)) for i in range(4)]
     m3 = m3 + squares
@@ -461,7 +452,7 @@
         w2 = spread(t, features[b], w2s[b])
         out[0, b] = ca * r0 - cb * w1
         out[1, b] = r0 - ca * w1 + cb * w2
-    drain()
+    sent("z2")
 
 
 def shards(probes, coords, features, noise_var, inv_scale, owner_map, block_pairs):
@@ -470,9 +461,6 @@
     out = pltpu.VMEM((2,) + probes.shape, F32)
     coords = jnp.transpose(coords, (1, 0, 2))
     block_pairs = jnp.transpose(block_pairs, (0, 2, 1))
-    pairs_of = []
-    for shape in ((15,), (16,), (4,), (3, 2, 2, 3), (16, 2), (7,), (15,), (8, 2), (15,)):
-        pairs_of += [dma(shape), dma(shape)]
     both = pl.pallas_call(
         kernel,
         out_shape=out,
@@ -511,10 +499,10 @@
             pltpu.VMEM((8, 8, 128), F32),
             pltpu.VMEM((2, 8, 128), F32),
             pltpu.VMEM((16, 8, 128), F32),
-            pltpu.VMEM((2, 8, 8, 128), F32),
+            pltpu.VMEM((16, 8, 128), F32),
             pltpu.VMEM((16, 8, 128), F32),
         ]
-        + pairs_of,
+        + [dma((len(GROUPS),))] * 2,
         compiler_params=pltpu.CompilerParams(
             collective_id=0, has_side_effects=True, vmem_limit_bytes=62 << 20
         ),

time: 55.6 us -> 53.2 us (0.957)
  Pallas kernels: 54.2 us -> 51.8 us
    pallas_call x1, Pallas kernels: 54.2 us -> 51.8 us  [shards(): pl.pallas_call(kernel, out_shape=out, in_specs=[pl.BlockSpec(memory_space...]
where the time goes in v5:
time: 53.2 us; the launch traced here: 53.1 us
  Pallas kernels  51.8 us (97%)
  between operations  0.64 us (1%)
  local copies, waits for them, and re-layouts  0.63 us (1%)
    pallas_call x1, Pallas kernels, shards(): pl.pallas_call(kernel, out_shape=out, in_specs=[pl.BlockSpec(memory_space...  51.8 us

profile of v5, /device:TPU:1, one launch (start us, length us, event | category | flops | bytes accessed | tf_op | source)
XLA Modules:
  0.0 53.1 jit_solution(12866477057433460268)
XLA Ops:
  0.6 51.8 %cg2.1 = f32[2,2,8,512]{3,2,1,0:T(8,128)S(1)} custom-call(f32[2,8,512]{2,1,0:T(8,128)} %probes_in.1, f32[3,2,512]{2,1,0:T(2,128)} %bitcast.6, f32[2,16,512]{2,1,0:T(8,128)} %features_in.1, f32[2,512]{1,0:T(2,128)} %noise_in.1, f32[3]{0:T(128)} %inv_scale_in.1, s32[1,64]{1,0:T(1,128)} %owner_in.1, s32[1,2,64]{2,1,0:T(2,128)} %bitcast.7), custom_call_target="tpu_custom_call" | custom-call | tf_op jit(solution)/shard_map/cg2/pallas_call | solution.py:464
  52.5 0.6 %slice_bitcast_fusion = (f32[2,8,512]{2,1,0:T(8,128)}, f32[2,8,512]{2,1,0:T(8,128)}) fusion(f32[2,2,8,512]{3,2,1,0:T(8,128)S(1)} %cg2.1), kind=kLoop, calls=%fused_computation | loop fusion | bytes 131072 | tf_op jit(solution)/shard_map/squeeze | solution.py:511

commit v6 on v5

--- a/solution.py
+++ b/solution.py
@@ -22,16 +22,14 @@
     "sib_loads",
     "forward",
     "a1",
-    "pair_first",
     "sib_diag",
-    "diag_first",
-    "pair_second",
-    "diag_second",
     "sib_w1",
     "a2",
     "results",
     "z2",
-)
+    "pairs",
+    "diag",
+) + tuple(n + str(h) + str(d) for n in ("pairs", "diag") for h in (0, 1) for d in (0, 1, 2))
 
 
 def kernel(
@@ -138,6 +136,28 @@
             for dy, dx in steps:
                 send(name, buf.at[span], buf.at[span], plane_peer(dy, dx, core))
         spans[name] = buf.at[pl.ds(0, 6 * m * (1 if stage_index == 0 else 4))]
+
+    def steps(h, first):
+        return [(0, d) if (h == 0) == first else (d, 0) for d in (1, 2, 3)]
+
+    def gather_start(name, buf, m, h):
+        own = buf.at[pl.ds(h * 16 * m + pos[h] * m, m)]
+        for d, step in enumerate(steps(h, True)):
+            send(name + str(h) + str(d), own, own, plane_peer(*step, core))
+            spans[name + str(h) + str(d)] = buf.at[pl.ds(0, m)]
+        for step in steps(h, False):
+            send(name, own, own, plane_peer(*step, core))
+
+    def gather_pass_on(name, buf, m):
+        for d in (0, 2, 1):
+            for h in (0, 1):
+                arrive(name + str(h) + str(d))
+                line, place = ((y, x), (x, y))[h]
+                at = h * 16 * m + (line * 4 + lax.rem(place + 3 - d, 4)) * m
+                span = buf.at[pl.ds(at, m)]
+                for step in steps(h, False):
+                    send(name, span, span, plane_peer(*step, core))
+        spans[name] = buf.at[pl.ds(0, 24 * m)]
 
     arrive("sib_field")
     gather_stage("field_first", field, 1, 0)
@@ -285,8 +305,9 @@
         ya = apply(split(vb), 2 + i, NT)
         yb = apply(split(va), 2 + i, NN)
         vp[(i // 2) * 32 + pos[i // 2] * 2 + i % 2] = jnp.where(low, ya, yb)
-
-    gather_stage("pair_first", vp, 2, 0)
+        if i % 2:
+            gather_start("pairs", vp, 2, i // 2)
+
 
     arrive("a1")
     g1 = ap1[0]
@@ -310,11 +331,10 @@
     c1 = jnp.where(core == 0, theirs, mine)
     vd[pos[0]] = jnp.where(low, c0, flip(c1))
     vd[16 + pos[1]] = jnp.where(low, flip(c0), c1)
-    gather_stage("diag_first", vd, 1, 0)
-    arrive("pair_first")
-    gather_stage("pair_second", vp, 2, 1)
-    arrive("diag_first")
-    gather_stage("diag_second", vd, 1, 1)
+    for h in (0, 1):
+        gather_start("diag", vd, 1, h)
+    gather_pass_on("pairs", vp, 2)
+    gather_pass_on("diag", vd, 1)
     j = lax.broadcasted_iota(jnp.int32, (1, 768), 1)
     n = j >> 3
     side = (j >> 2) & 1
@@ -342,9 +362,11 @@
     row32 = lax.broadcasted_iota(jnp.int32, (256, 32), 0)
     w3 = jnp.where((slot32 == (row32 >> 2)) & ((lane32 & 3) == (row32 & 3)), 1.0, 0.0).astype(BF16)
     sent("sib_field", "points", "field_first", "z1", "field_second", "sib_loads", "forward", "a1")
-    sent("pair_first", "sib_diag", "diag_first")
-    arrive("pair_second")
-    arrive("diag_second")
+    sent("sib_diag")
+    for name in ("pairs", "diag"):
+        sent(*(name + str(h) + str(d) for h in (0, 1) for d in (0, 1, 2)))
+    arrive("pairs")
+    arrive("diag")
 
     acc = None
     for lo_row in range(0, 768, 256):
@@ -407,7 +429,7 @@
             send("results", dense.at[plane_chip(dy, dx), cc], landed.at[here], plane_peer(dy, dx, cc))
     spans["results"] = landed.at[pl.ds(0, 31)]
 
-    sent("pair_second", "diag_second", "sib_w1")
+    sent("pairs", "diag", "sib_w1")
     arrive("a2")
     t = ap2[0]
     for i in range(1, 16):

time: 53.2 us -> 50.8 us (0.955)
  Pallas kernels: 51.8 us -> 49.4 us
    pallas_call x1, Pallas kernels: 51.8 us -> 49.4 us  [shards(): pl.pallas_call(kernel, out_shape=out, in_specs=[pl.BlockSpec(memory_space...]
where the time goes in v6:
time: 50.8 us; the launch traced here: 50.7 us
  Pallas kernels  49.4 us (97%)
  between operations  0.64 us (1%)
  local copies, waits for them, and re-layouts  0.63 us (1%)
    pallas_call x1, Pallas kernels, shards(): pl.pallas_call(kernel, out_shape=out, in_specs=[pl.BlockSpec(memory_space...  49.4 us

profile of v6, /device:TPU:1, one launch (start us, length us, event | category | flops | bytes accessed | tf_op | source)
XLA Modules:
  0.0 50.7 jit_solution(14639685081908188880)
XLA Ops:
  0.6 49.4 %cg2.1 = f32[2,2,8,512]{3,2,1,0:T(8,128)S(1)} custom-call(f32[2,8,512]{2,1,0:T(8,128)} %probes_in.1, f32[3,2,512]{2,1,0:T(2,128)} %bitcast.6, f32[2,16,512]{2,1,0:T(8,128)} %features_in.1, f32[2,512]{1,0:T(2,128)} %noise_in.1, f32[3]{0:T(128)} %inv_scale_in.1, s32[1,64]{1,0:T(1,128)} %owner_in.1, s32[1,2,64]{2,1,0:T(2,128)} %bitcast.7), custom_call_target="tpu_custom_call" | custom-call | tf_op jit(solution)/shard_map/cg2/pallas_call | solution.py:486
  50.0 0.6 %slice_bitcast_fusion = (f32[2,8,512]{2,1,0:T(8,128)}, f32[2,8,512]{2,1,0:T(8,128)}) fusion(f32[2,2,8,512]{3,2,1,0:T(8,128)S(1)} %cg2.1), kind=kLoop, calls=%fused_computation | loop fusion | bytes 131072 | tf_op jit(solution)/shard_map/squeeze | solution.py:533

commit v7 on v6

--- a/solution.py
+++ b/solution.py
@@ -36,7 +36,7 @@
     probes_in, coords_in, features_in, noise_in, inv_scale_in, owner_in, pairs_in,
     out,
     probes, coords, features, noise, inv_scale, owner_s, pairs_s, owner_v, pairs_v, in_sem,
-    points, field, halves, cross, sib_cross, vp, vd, dense, landed, kh, kl, turned, fh, fl, w2f, w2b, diag, targets,
+    points, field, halves, cross, sib_cross, vp, vd, dense, landed, kh, kl, turned, left_terms, fh, fl, w2f, w2b, diag, targets,
     tile, az1, ac1, ap1, az2, ap2,
     group_send, group_recv,
 ):
@@ -95,6 +95,31 @@
     halves[1] = jnp.where(low, flip(p0), p1)
     field[core * 16 + lax.select(core == 0, pos[0], pos[1])] = halves[core]
 
+    for c in loads_in[3:]:
+        c.wait()
+    for b in (0, 1):
+        f = features[b]
+        high = f.astype(BF16)
+        fh[b] = high
+        fl[b] = (f - high.astype(F32)).astype(BF16)
+
+    def stack(v):
+        top = v.astype(BF16).astype(F32)
+        return jnp.concatenate([top, v - top], axis=0).astype(BF16)
+
+    def unstack(v, high, rest, dims):
+        d = lax.dot_general(v, high, dims, preferred_element_type=F32)
+        d = d + lax.dot_general(v, rest, dims, preferred_element_type=F32)
+        return d[0:8] + d[8:16]
+
+    def loads(v0, v1):
+        tile[:, 0:16] = unstack(v0, fh[0], fl[0], NT) + unstack(v1, fh[1], fl[1], NT)
+        return tile[...]
+
+    tile[...] = jnp.zeros_like(tile)
+    first_stack = [stack(probes[b]) for b in (0, 1)]
+    az1[region] = loads(*first_stack)
+
     pl.semaphore_wait(barrier, 23)
 
     def send(group, src, dst, device):
@@ -121,6 +146,9 @@
     own_field = field.at[core * 16 + lax.select(core == 0, pos[0], pos[1])]
     send("sib_field", halves.at[other], own_field, sibling)
     spans["sib_field"] = halves.at[0]
+    for d in range(1, 8):
+        send("z1", az1.at[region], az1.at[region], z_peer(d, core))
+    spans["z1"] = az1.at[pl.ds(0, 7)]
     for dy, dx in PLANE:
         send("points", points.at[here], points.at[here], plane_peer(dy, dx, core))
     spans["points"] = points.at[pl.ds(0, 15)]
@@ -162,21 +190,37 @@
     arrive("sib_field")
     gather_stage("field_first", field, 1, 0)
 
-    for c in loads_in[3:]:
-        c.wait()
     sx, sy, st = inv_scale[0], inv_scale[1], inv_scale[2]
 
+    one = jnp.ones((1, BLK), F32)
+
+    def parts(v):
+        top = v.astype(BF16).astype(F32)
+        mid = (v - top).astype(BF16).astype(F32)
+        return top, mid, v - top - mid
+
     def make_tile(index, left, right):
-        turned[...] = jnp.transpose(left)
-        rx, ry, rt = right[0:1, :] * sx, right[1:2, :] * sy, right[2:3, :] * st
+        lt_rows, rt_rows = [], []
+        for i, scale in ((0, sx), (1, sy)):
+            h, m, l = parts((left[i : i + 1, :] - 0.5) * scale)
+            rh, rm, rl = parts((right[i : i + 1, :] - 0.5) * scale)
+            lt_rows += [-2.0 * h, -2.0 * h, -2.0 * m, -2.0 * h, -2.0 * l, -2.0 * m]
+            rt_rows += [rh, rm, rh, rl, rh, rm]
+        for v, rows, is_left in ((left, lt_rows, True), (right, rt_rows, False)):
+            a, b = (v[0:1, :] - 0.5) * sx, (v[1:2, :] - 0.5) * sy
+            n = list(parts(a * a + b * b))
+            rows += n + [one] * 3 if is_left else [one] * 3 + n
+        t = jnp.transpose(jnp.concatenate(lt_rows + [jnp.zeros((6, BLK), F32), left], axis=0))
+        turned[...] = t
+        rm_all = jnp.concatenate(rt_rows + [jnp.zeros((14, BLK), F32)], axis=0).astype(BF16)
+        left_terms[...] = jnp.where(lax.broadcasted_iota(jnp.int32, (BLK, 32), 1) < 18, t, 0.0).astype(BF16)
+        rt = right[2:3, :] * st
 
         def rows(i, _):
-            span = pl.ds(pl.multiple_of(i * 16, 16), 16)
-            part = turned[span, :]
-            dx = part[:, 0:1] * sx - rx
-            dy = part[:, 1:2] * sy - ry
-            dt = part[:, 2:3] * st - rt
-            sq = jnp.maximum(dx * dx + dy * dy, 1e-30)
+            span = pl.ds(pl.multiple_of(i * 128, 128), 128)
+            sq = lax.dot_general(left_terms[span, :], rm_all, NN, preferred_element_type=F32)
+            dt = turned[span, 26:27] * st - rt
+            sq = jnp.maximum(sq, 1e-30)
             a = jnp.maximum(1.0 - sq * lax.rsqrt(sq), 0.0)
             b = jnp.maximum(1.0 - jnp.abs(dt), 0.0)
             m = a * b
@@ -188,7 +232,7 @@
             kl[index, span, :] = (value - high.astype(F32)).astype(BF16)
             return 0
 
-        lax.fori_loop(0, 32, rows, 0, unroll=32)
+        lax.fori_loop(0, 4, rows, 0, unroll=4)
 
     def points_of(index, b):
         v = points[index]
@@ -215,32 +259,6 @@
 
     def apply(v, index, dims):
         return 4.0 * fold(v, kh[index], kl[index], dims)
-
-    for b in (0, 1):
-        f = features[b]
-        high = f.astype(BF16)
-        fh[b] = high
-        fl[b] = (f - high.astype(F32)).astype(BF16)
-
-    def stack(v):
-        top = v.astype(BF16).astype(F32)
-        return jnp.concatenate([top, v - top], axis=0).astype(BF16)
-
-    def unstack(v, high, rest, dims):
-        d = lax.dot_general(v, high, dims, preferred_element_type=F32)
-        d = d + lax.dot_general(v, rest, dims, preferred_element_type=F32)
-        return d[0:8] + d[8:16]
-
-    def loads(v0, v1):
-        tile[:, 0:16] = unstack(v0, fh[0], fl[0], NT) + unstack(v1, fh[1], fl[1], NT)
-        return tile[...]
-
-    tile[...] = jnp.zeros_like(tile)
-    first_stack = [stack(probes[b]) for b in (0, 1)]
-    az1[region] = loads(*first_stack)
-    for d in range(1, 8):
-        send("z1", az1.at[region], az1.at[region], z_peer(d, core))
-    spans["z1"] = az1.at[pl.ds(0, 7)]
 
     mine0 = points[here]
     make_tile(0, mine0, mine0)
@@ -365,11 +383,13 @@
     sent("sib_diag")
     for name in ("pairs", "diag"):
         sent(*(name + str(h) + str(d) for h in (0, 1) for d in (0, 1, 2)))
+    square = jnp.sum(probes[0] * probes[0] + probes[1] * probes[1], axis=1, keepdims=True)
     arrive("pairs")
-    arrive("diag")
 
     acc = None
     for lo_row in range(0, 768, 256):
+        if lo_row == 512:
+            arrive("diag")
         part = vp[lo_row // 8 : lo_row // 8 + 32] if lo_row < 512 else vd[...]
         part = part.reshape(256, BLK)
         w = w2b[:, lo_row : lo_row + 256]
@@ -395,18 +415,18 @@
     c1 = jnp.where(core == 0, theirs, mine)
     w1s = [jnp.where(low, c0, flip(c1)), jnp.where(low, flip(c0), c1)]
     stacks = [stack(w) for w in w1s]
-    dot00, dot01, dot11 = jnp.zeros((8, BLK), F32), jnp.zeros((8, BLK), F32), jnp.zeros((8, BLK), F32)
+    dot01, dot11 = jnp.zeros((8, BLK), F32), jnp.zeros((8, BLK), F32)
     for b in (0, 1):
         r0, w1 = probes[b], w1s[b]
         z = factor[b] * (4.0 * unstack(stacks[b], kh[b], kl[b], NN)) + noise[b : b + 1, :] * w1
         diag[b] = z
         form = form + w1 * z
-        dot00 = dot00 + r0 * r0
         dot01 = dot01 + r0 * w1
         dot11 = dot11 + w1 * w1
     stats = loads(*stacks)
-    for i, v in enumerate((dot01, dot11, form, dot00)):
+    for i, v in enumerate((dot01, dot11, form)):
         stats = jnp.where(lane == 16 + i, jnp.sum(v, axis=1, keepdims=True), stats)
+    stats = jnp.where(lane == 19, square, stats)
     ap2[chip] = stats
     for dy, dx in PLANE:
         send("a2", ap2.at[chip], ap2.at[chip], plane_peer(dy, dx, core))
@@ -510,7 +530,8 @@
             pltpu.VMEM((32, 8, BLK), F32),
             pltpu.VMEM((6, BLK, BLK), BF16),
             pltpu.VMEM((6, BLK, BLK), BF16),
-            pltpu.VMEM((BLK, 8), F32),
+            pltpu.VMEM((BLK, 32), F32),
+            pltpu.VMEM((BLK, 32), BF16),
             pltpu.VMEM((2, 16, BLK), BF16),
             pltpu.VMEM((2, 16, BLK), BF16),
             pltpu.VMEM((80, 768), F32),

time: 50.8 us -> 50.2 us (0.988)
  Pallas kernels: 49.4 us -> 48.8 us
    pallas_call x1, Pallas kernels: 49.4 us -> 48.8 us  [shards(): pl.pallas_call(kernel, out_shape=out, in_specs=[pl.BlockSpec(memory_space...]
where the time goes in v7:
time: 50.2 us; the launch traced here: 50.1 us
  Pallas kernels  48.8 us (97%)
  between operations  0.64 us (1%)
  local copies, waits for them, and re-layouts  0.63 us (1%)
    pallas_call x1, Pallas kernels, shards(): pl.pallas_call(kernel, out_shape=out, in_specs=[pl.BlockSpec(memory_space...  48.8 us

profile of v7, /device:TPU:1, one launch (start us, length us, event | category | flops | bytes accessed | tf_op | source)
XLA Modules:
  0.0 50.1 jit_solution(5306217560584559728)
XLA Ops:
  0.6 48.8 %cg2.1 = f32[2,2,8,512]{3,2,1,0:T(8,128)S(1)} custom-call(f32[2,8,512]{2,1,0:T(8,128)} %probes_in.1, f32[3,2,512]{2,1,0:T(2,128)} %bitcast.6, f32[2,16,512]{2,1,0:T(8,128)} %features_in.1, f32[2,512]{1,0:T(2,128)} %noise_in.1, f32[3]{0:T(128)} %inv_scale_in.1, s32[1,64]{1,0:T(1,128)} %owner_in.1, s32[1,2,64]{2,1,0:T(2,128)} %bitcast.7), custom_call_target="tpu_custom_call" | custom-call | tf_op jit(solution)/shard_map/cg2/pallas_call | solution.py:506
  49.4 0.6 %slice_bitcast_fusion = (f32[2,8,512]{2,1,0:T(8,128)}, f32[2,8,512]{2,1,0:T(8,128)}) fusion(f32[2,2,8,512]{3,2,1,0:T(8,128)S(1)} %cg2.1), kind=kLoop, calls=%fused_computation | loop fusion | bytes 131072 | tf_op jit(solution)/shard_map/squeeze | solution.py:554
